TPU v7x, 256 devices: a whole 4x4x8 slice. The times are simulated.
256 devices in a mesh: pipe: 4 (over x), expert: 64 (over z, y, core).
Axes of the slice: x: 4, y: 4, z: 8, core: 2. Of those that a mesh axis runs over, the one named last changes fastest.
Arguments:
- cotangent: bfloat16 [2, 4096, 1024], P(None, 'expert'), may hold values from -6 to 6
- expert_ids: int32 [4, 2, 4096, 6], P('pipe', None, 'expert'), may hold values from 0 to 63, all different within a row; in each aligned block of 64 rows (0 to 63, 64 to 127, ..., all dimensions but the last counted through in order) at most 7 rows name the same one
- gates: float32 [4, 2, 4096, 6], P('pipe', None, 'expert'), may hold values from 0.03 to 0.5
- layer_inputs: bfloat16 [4, 2, 4096, 1024], P('pipe', None, 'expert'), may hold values from -3 to 3
- saved_fc1: bfloat16 [4, 2, 64, 448, 1408], P('pipe', None, 'expert'), may hold values from -6 to 6
- w_fc1: bfloat16 [4, 64, 1024, 1408], P('pipe', 'expert'), may hold values from -0.1875 to 0.1875
- w_fc2: bfloat16 [4, 64, 704, 1024], P('pipe', 'expert'), may hold values from -0.21875 to 0.21875
Outputs:
- section_grads: bfloat16 [4, 2, 4096, 1024], P('pipe', None, 'expert')
- fc1_grad: bfloat16 [4, 64, 1024, 1408], P('pipe', 'expert')
- fc2_grad: bfloat16 [4, 64, 704, 1024], P('pipe', 'expert')
Inputs may be any that keep to these rules, and one draw needn't show every extreme that they name: `expert_ids`: each token names 6 different experts; in each section, micro-batch and aligned block of 64 tokens no expert is named by more than 7 tokens.
All inputs are finite; a program needn't handle non-finite values.
Results may differ from a plain program's by a relative error of at most 0.015.
Values may be sent and summed in bfloat16 or wider, within the bound.
A program may use at most 128 MiB of HBM per device.

v0:
```python
import jax
import jax.numpy as jnp
from jax import lax
from jax.sharding import PartitionSpec as P


def shifted(value, axis, by):
    length = lax.axis_size(axis)
    pairs = [(i, i + by) for i in range(length) if 0 <= i + by < length]
    return lax.ppermute(value, axis, pairs)


def slot_targets(expert_now, expert_count, capacity):
    flat_ids = expert_now.reshape(-1)
    pair_count = flat_ids.shape[0]
    onehot = (flat_ids[:, None] == jnp.arange(expert_count, dtype=jnp.int32)[None, :]).astype(
        jnp.float32
    )
    row_iota = lax.broadcasted_iota(jnp.int32, (pair_count, pair_count), 0)
    col_iota = lax.broadcasted_iota(jnp.int32, (pair_count, pair_count), 1)
    lower_mask = (col_iota < row_iota).astype(jnp.float32)
    rank_count = jnp.dot(
        lower_mask, onehot, precision=lax.Precision.HIGHEST, preferred_element_type=jnp.float32
    )
    slot_index = jnp.sum(rank_count * onehot, axis=1).astype(jnp.int32)
    return flat_ids * capacity + slot_index


def expert_grads(routed, fc1_now, weight_one, weight_two):
    hidden_width = weight_two.shape[0]
    hidden_grad = lax.dot_general(
        routed, weight_two, (((1,), (1,)), ((), ())), preferred_element_type=jnp.float32
    )
    pre_gate = fc1_now[:, :hidden_width].astype(jnp.float32)
    pre_up = fc1_now[:, hidden_width:].astype(jnp.float32)
    sigmoid_v = jax.nn.sigmoid(pre_gate)
    gate_part = (hidden_grad * pre_up * (sigmoid_v * (1.0 + pre_gate * (1.0 - sigmoid_v)))).astype(
        jnp.bfloat16
    )
    up_part = (hidden_grad * (pre_gate * sigmoid_v)).astype(jnp.bfloat16)
    fc1_out_grad = jnp.concatenate([gate_part, up_part], axis=1)
    row_grads = lax.dot_general(
        fc1_out_grad, weight_one, (((1,), (1,)), ((), ())), preferred_element_type=jnp.float32
    )
    return (fc1_out_grad, row_grads.astype(jnp.bfloat16))


def store_at(store, value, micro_idx, is_valid):
    previous = lax.dynamic_index_in_dim(store, micro_idx, 0, keepdims=False)
    return lax.dynamic_update_index_in_dim(
        store, jnp.where(is_valid, value, previous), micro_idx, 0
    )


def per_device(cotangent, expert_ids, gates, layer_inputs, saved_fc1, w_fc1, w_fc2):
    expert_count = lax.axis_size("expert")
    sections = lax.axis_size("pipe")
    my_section = lax.axis_index("pipe")
    micro_count, tok_rows, model_width = cotangent.shape
    top_k = expert_ids.shape[3]
    slot_count = saved_fc1.shape[3]
    capacity = slot_count // expert_count
    hidden = w_fc2.shape[2]
    weight_one = w_fc1[0, 0]
    weight_two = w_fc2[0, 0]
    fc1_local = saved_fc1[0, :, 0]

    def placement(micro_idx):
        expert_now = lax.dynamic_index_in_dim(expert_ids[0], micro_idx, 0, keepdims=False)
        return slot_targets(expert_now, expert_count, capacity)

    def spread(row_block, target):
        filled = (
            jnp.zeros((expert_count * capacity, model_width), jnp.bfloat16)
            .at[target]
            .set(row_block)
        )
        return filled.reshape(expert_count, capacity, model_width)

    grad_store = jnp.zeros((micro_count, slot_count, model_width), jnp.bfloat16)
    fc1g_store = jnp.zeros((micro_count, slot_count, 2 * hidden), jnp.bfloat16)
    section_out = jnp.zeros((micro_count, tok_rows, model_width), jnp.bfloat16)
    plan = [tick_no - (sections - 1 - my_section) for tick_no in range(sections + micro_count - 1)]
    received = jnp.zeros((tok_rows, model_width), jnp.bfloat16)
    for turn_idx in range(len(plan)):
        raw_micro = jnp.asarray(plan[turn_idx], jnp.int32)
        is_valid = (raw_micro >= 0) & (raw_micro < micro_count)
        micro_idx = jnp.clip(raw_micro, 0, micro_count - 1)
        grad_in = jnp.where(
            my_section == sections - 1,
            lax.dynamic_index_in_dim(cotangent, micro_idx, 0, keepdims=False),
            received,
        )
        target = placement(micro_idx)
        gate_now = lax.dynamic_index_in_dim(gates[0], micro_idx, 0, keepdims=False)
        scaled_rows = (gate_now[:, :, None] * grad_in[:, None, :].astype(jnp.float32)).astype(
            jnp.bfloat16
        )
        outgoing = spread(scaled_rows.reshape(tok_rows * top_k, model_width), target)
        routed = lax.all_to_all(outgoing, "expert", split_axis=0, concat_axis=0, tiled=True)
        routed = routed.reshape(slot_count, model_width)
        fc1_now = lax.dynamic_index_in_dim(fc1_local, micro_idx, 0, keepdims=False)
        fc1_out_grad, row_grads = lax.cond(
            is_valid,
            lambda: expert_grads(routed, fc1_now, weight_one, weight_two),
            lambda: (
                jnp.zeros((slot_count, 2 * hidden), jnp.bfloat16),
                jnp.zeros((slot_count, model_width), jnp.bfloat16),
            ),
        )
        returned = lax.all_to_all(
            row_grads.reshape(expert_count, capacity, model_width),
            "expert",
            split_axis=0,
            concat_axis=0,
            tiled=True,
        )
        picked = (
            returned.reshape(slot_count, model_width)[target]
            .reshape(tok_rows, top_k, model_width)
            .astype(jnp.float32)
        )
        grad_out = (grad_in.astype(jnp.float32) + jnp.sum(picked, axis=1)).astype(jnp.bfloat16)
        grad_store = store_at(grad_store, routed, micro_idx, is_valid)
        fc1g_store = store_at(fc1g_store, fc1_out_grad, micro_idx, is_valid)
        section_out = store_at(section_out, grad_out, micro_idx, is_valid)
        if turn_idx + 1 < len(plan):
            received = shifted(grad_out, "pipe", -1)
    acc_one = jnp.zeros((model_width, 2 * hidden), jnp.float32)
    acc_two = jnp.zeros((hidden, model_width), jnp.float32)
    for micro_no in range(micro_count):
        target = placement(micro_no)
        token_rows = lax.dynamic_index_in_dim(layer_inputs[0], micro_no, 0, keepdims=False)
        repeated = jnp.broadcast_to(token_rows[:, None, :], (tok_rows, top_k, model_width)).reshape(
            tok_rows * top_k, model_width
        )
        routed_x = lax.all_to_all(
            spread(repeated, target), "expert", split_axis=0, concat_axis=0, tiled=True
        ).reshape(slot_count, model_width)
        fc1_now = fc1_local[micro_no]
        pre_gate = fc1_now[:, :hidden].astype(jnp.float32)
        pre_up = fc1_now[:, hidden:].astype(jnp.float32)
        activation = (pre_gate * jax.nn.sigmoid(pre_gate) * pre_up).astype(jnp.bfloat16)
        acc_two = acc_two + lax.dot_general(
            activation,
            grad_store[micro_no],
            (((0,), (0,)), ((), ())),
            preferred_element_type=jnp.float32,
        )
        acc_one = acc_one + lax.dot_general(
            routed_x,
            fc1g_store[micro_no],
            (((0,), (0,)), ((), ())),
            preferred_element_type=jnp.float32,
        )
    return (
        section_out[None],
        acc_one.astype(jnp.bfloat16)[None, None],
        acc_two.astype(jnp.bfloat16)[None, None],
    )


def solution(mesh):
    in_specs = (
        P(None, "expert", None),
        P("pipe", None, "expert", None),
        P("pipe", None, "expert", None),
        P("pipe", None, "expert", None),
        P("pipe", None, "expert", None, None),
        P("pipe", "expert", None, None),
        P("pipe", "expert", None, None),
    )
    out_specs = (
        P("pipe", None, "expert", None),
        P("pipe", "expert", None, None),
        P("pipe", "expert", None, None),
    )
    return jax.shard_map(
        per_device, mesh=mesh, in_specs=in_specs, out_specs=out_specs, check_vma=False
    )
```

profile of v0, /device:TPU:1, one launch (start us, length us, event | category | flops | bytes accessed | tf_op | source)
XLA Modules:
  0.0 576.5 jit_solution(12867243947233437860)
XLA Ops:
  11.5 13.3 %all-to-all-start = ((bf16[64,7,1024]{2,1,0:T(8,128)(2,1)}), bf16[64,7,1024]{2,1,0:T(8,128)(2,1)}, u32[]{:S(2)}, u32[]{:S(2)}) async-start(bf16[64,7,1024]{2,1,0:T(8,128)(2,1)} %reshape.486), calls=%async_computation | async-start | bytes 2097152 | tf_op jit(solution)/shard_map/all_to_all | solution.py:100
  24.9 27.9 %all-to-all-done = bf16[64,7,1024]{2,1,0:T(8,128)(2,1)} async-done(((bf16[64,7,1024]{2,1,0:T(8,128)(2,1)}), bf16[64,7,1024]{2,1,0:T(8,128)(2,1)}, u32[]{:S(2)}, u32[]{:S(2)}) %all-to-all-start) | async-done | bytes 917536 | tf_op jit(solution)/shard_map/all_to_all | solution.py:100
  55.3 6.7 %all-to-all-start.1 = ((bf16[64,7,1024]{2,1,0:T(8,128)(2,1)}), bf16[64,7,1024]{2,1,0:T(8,128)(2,1)}, u32[]{:S(2)}, u32[]{:S(2)}) async-start(bf16[64,7,1024]{2,1,0:T(8,128)(2,1)} %reshape.487), calls=%async_computation.1 | async-start | bytes 2097152 | tf_op jit(solution)/shard_map/all_to_all | solution.py:111
  61.9 27.9 %all-to-all-done.1 = bf16[64,7,1024]{2,1,0:T(8,128)(2,1)} async-done(((bf16[64,7,1024]{2,1,0:T(8,128)(2,1)}), bf16[64,7,1024]{2,1,0:T(8,128)(2,1)}, u32[]{:S(2)}, u32[]{:S(2)}) %all-to-all-start.1) | async-done | bytes 917536 | tf_op jit(solution)/shard_map/all_to_all | solution.py:111
  114.1 7.9 %all-to-all-start.2 = ((bf16[64,7,1024]{2,1,0:T(8,128)(2,1)}), bf16[64,7,1024]{2,1,0:T(8,128)(2,1)}, u32[]{:S(2)}, u32[]{:S(2)}) async-start(bf16[64,7,1024]{2,1,0:T(8,128)(2,1)} %reshape.489), calls=%async_computation.2 | async-start | bytes 2097152 | tf_op jit(solution)/shard_map/all_to_all | solution.py:100
  122.0 27.9 %all-to-all-done.2 = bf16[64,7,1024]{2,1,0:T(8,128)(2,1)} async-done(((bf16[64,7,1024]{2,1,0:T(8,128)(2,1)}), bf16[64,7,1024]{2,1,0:T(8,128)(2,1)}, u32[]{:S(2)}, u32[]{:S(2)}) %all-to-all-start.2) | async-done | bytes 917536 | tf_op jit(solution)/shard_map/all_to_all | solution.py:100
  152.5 6.8 %all-to-all-start.3 = ((bf16[64,7,1024]{2,1,0:T(8,128)(2,1)}), bf16[64,7,1024]{2,1,0:T(8,128)(2,1)}, u32[]{:S(2)}, u32[]{:S(2)}) async-start(bf16[64,7,1024]{2,1,0:T(8,128)(2,1)} %reshape.490), calls=%async_computation.3 | async-start | bytes 2097152 | tf_op jit(solution)/shard_map/all_to_all | solution.py:111
  161.4 25.7 %all-to-all-done.3 = bf16[64,7,1024]{2,1,0:T(8,128)(2,1)} async-done(((bf16[64,7,1024]{2,1,0:T(8,128)(2,1)}), bf16[64,7,1024]{2,1,0:T(8,128)(2,1)}, u32[]{:S(2)}, u32[]{:S(2)}) %all-to-all-start.3) | async-done | bytes 917536 | tf_op jit(solution)/shard_map/all_to_all | solution.py:111
  215.6 7.9 %all-to-all-start.4 = ((bf16[64,7,1024]{2,1,0:T(8,128)(2,1)}), bf16[64,7,1024]{2,1,0:T(8,128)(2,1)}, u32[]{:S(2)}, u32[]{:S(2)}) async-start(bf16[64,7,1024]{2,1,0:T(8,128)(2,1)} %reshape.492), calls=%async_computation.4 | async-start | bytes 2097152 | tf_op jit(solution)/shard_map/all_to_all | solution.py:100
  223.5 27.9 %all-to-all-done.4 = bf16[64,7,1024]{2,1,0:T(8,128)(2,1)} async-done(((bf16[64,7,1024]{2,1,0:T(8,128)(2,1)}), bf16[64,7,1024]{2,1,0:T(8,128)(2,1)}, u32[]{:S(2)}, u32[]{:S(2)}) %all-to-all-start.4) | async-done | bytes 917536 | tf_op jit(solution)/shard_map/all_to_all | solution.py:100
  255.8 6.8 %all-to-all-start.5 = ((bf16[64,7,1024]{2,1,0:T(8,128)(2,1)}), bf16[64,7,1024]{2,1,0:T(8,128)(2,1)}, u32[]{:S(2)}, u32[]{:S(2)}) async-start(bf16[64,7,1024]{2,1,0:T(8,128)(2,1)} %reshape.493), calls=%async_computation.5 | async-start | bytes 2097152 | tf_op jit(solution)/shard_map/all_to_all | solution.py:111
  274.5 16.1 %all-to-all-done.5 = bf16[64,7,1024]{2,1,0:T(8,128)(2,1)} async-done(((bf16[64,7,1024]{2,1,0:T(8,128)(2,1)}), bf16[64,7,1024]{2,1,0:T(8,128)(2,1)}, u32[]{:S(2)}, u32[]{:S(2)}) %all-to-all-start.5) | async-done | bytes 917536 | tf_op jit(solution)/shard_map/all_to_all | solution.py:111
  290.5 6.7 %all-to-all-start.10 = ((bf16[64,7,1024]{2,1,0:T(8,128)(2,1)}), bf16[64,7,1024]{2,1,0:T(8,128)(2,1)}, u32[]{:S(2)}, u32[]{:S(2)}) async-start(bf16[64,7,1024]{2,1,0:T(8,128)(2,1)} %reshape.502), calls=%async_computation.10 | async-start | bytes 2097152 | tf_op jit(solution)/shard_map/all_to_all | solution.py:137
  310.7 31.6 %collective-permute-done.2 = bf16[64,1024]{1,0:T(8,128)(2,1)S(1)} collective-permute-done((bf16[64,1024]{1,0:T(8,128)(2,1)}, bf16[64,1024]{1,0:T(8,128)(2,1)S(1)}, u32[]{:S(2)}, u32[]{:S(2)}) %collective-permute-start.2) | collective-permute-done | bytes 131104 | tf_op jit(solution)/shard_map/ppermute | solution.py:10
  353.7 11.3 %all-to-all-start.6 = ((bf16[64,7,1024]{2,1,0:T(8,128)(2,1)}), bf16[64,7,1024]{2,1,0:T(8,128)(2,1)}, u32[]{:S(2)}, u32[]{:S(2)}) async-start(bf16[64,7,1024]{2,1,0:T(8,128)(2,1)} %reshape.495), calls=%async_computation.6 | async-start | bytes 2097152 | tf_op jit(solution)/shard_map/all_to_all | solution.py:100
  375.0 17.9 %all-to-all-done.6 = bf16[64,7,1024]{2,1,0:T(8,128)(2,1)} async-done(((bf16[64,7,1024]{2,1,0:T(8,128)(2,1)}), bf16[64,7,1024]{2,1,0:T(8,128)(2,1)}, u32[]{:S(2)}, u32[]{:S(2)}) %all-to-all-start.6) | async-done | bytes 917536 | tf_op jit(solution)/shard_map/all_to_all | solution.py:100
  404.8 12.2 %conditional.8 = (bf16[448,1408]{1,0:T(8,128)(2,1)}, bf16[448,1024]{1,0:T(8,128)(2,1)}) conditional(s32[]{:T(128)} %convert_element_type.375, () %tuple.64, (bf16[64,7,1024]{2,1,0:T(8,128)(2,1)}, bf16[704,1024]{1,0:T(8,128)(2,1)}, bf16[1,2,1,448,1408]{4,3,2,1,0:T(8,128)(2,1)S(1)}, s32[]{:T(128)}, bf16[1024,1408]{1,0:T(8,128)(2,1)}) %tuple.115), branch_computations={%region_17.18_spmd, %region_18.19_spmd} | conditional | flops 1945481216 | bytes 28360752 | solution.py:103
  419.2 8.4 %all-to-all-done.11 = bf16[64,7,1024]{2,1,0:T(8,128)(2,1)} async-done(((bf16[64,7,1024]{2,1,0:T(8,128)(2,1)}), bf16[64,7,1024]{2,1,0:T(8,128)(2,1)}, u32[]{:S(2)}, u32[]{:S(2)}) %all-to-all-start.11) | async-done | bytes 917536 | tf_op jit(solution)/shard_map/all_to_all | solution.py:137
  452.2 10.0 %all-to-all-done.7 = bf16[64,7,1024]{2,1,0:T(8,128)(2,1)} async-done(((bf16[64,7,1024]{2,1,0:T(8,128)(2,1)}), bf16[64,7,1024]{2,1,0:T(8,128)(2,1)}, u32[]{:S(2)}, u32[]{:S(2)}) %all-to-all-start.7) | async-done | bytes 917536 | tf_op jit(solution)/shard_map/all_to_all | solution.py:111
  487.6 7.9 %all-to-all-start.8 = ((bf16[64,7,1024]{2,1,0:T(8,128)(2,1)}), bf16[64,7,1024]{2,1,0:T(8,128)(2,1)}, u32[]{:S(2)}, u32[]{:S(2)}) async-start(bf16[64,7,1024]{2,1,0:T(8,128)(2,1)} %reshape.498), calls=%async_computation.8 | async-start | bytes 2097152 | tf_op jit(solution)/shard_map/all_to_all | solution.py:100
  515.5 7.9 %all-to-all-done.8 = bf16[64,7,1024]{2,1,0:T(8,128)(2,1)} async-done(((bf16[64,7,1024]{2,1,0:T(8,128)(2,1)}), bf16[64,7,1024]{2,1,0:T(8,128)(2,1)}, u32[]{:S(2)}, u32[]{:S(2)}) %all-to-all-start.8) | async-done | bytes 917536 | tf_op jit(solution)/shard_map/all_to_all | solution.py:100
  523.4 9.9 %conditional.9 = (bf16[448,1408]{1,0:T(8,128)(2,1)}, bf16[448,1024]{1,0:T(8,128)(2,1)S(1)}) conditional(s32[]{:T(128)} %convert_element_type.383, () %tuple.66, (bf16[64,7,1024]{2,1,0:T(8,128)(2,1)}, bf16[704,1024]{1,0:T(8,128)(2,1)}, bf16[1,2,1,448,1408]{4,3,2,1,0:T(8,128)(2,1)S(1)}, s32[]{:T(128)}, bf16[1024,1408]{1,0:T(8,128)(2,1)}) %tuple.116), branch_computations={%region_22.23_spmd, %region_23.24_spmd} | conditional | flops 1945481216 | bytes 33407052 | solution.py:103
  534.6 7.1 %all-to-all-start.9 = ((bf16[64,7,1024]{2,1,0:T(8,128)(2,1)}), bf16[64,7,1024]{2,1,0:T(8,128)(2,1)}, u32[]{:S(2)}, u32[]{:S(2)}) async-start(bf16[64,7,1024]{2,1,0:T(8,128)(2,1)} %reshape.499), calls=%async_computation.9 | async-start | bytes 2097152 | tf_op jit(solution)/shard_map/all_to_all | solution.py:111
  560.4 9.0 %all-to-all-done.9 = bf16[64,7,1024]{2,1,0:T(8,128)(2,1)} async-done(((bf16[64,7,1024]{2,1,0:T(8,128)(2,1)}), bf16[64,7,1024]{2,1,0:T(8,128)(2,1)}, u32[]{:S(2)}, u32[]{:S(2)}) %all-to-all-start.9) | async-done | bytes 917536 | tf_op jit(solution)/shard_map/all_to_all | solution.py:111
  (276 shorter events, 259.1 us)
Async XLA Ops:
  10.2 42.5 %copy-start = (bf16[1,2,1,448,1408]{4,3,2,1,0:T(8,128)(2,1)S(1)}, bf16[1,2,1,448,1408]{4,3,2,1,0:T(8,128)(2,1)}, u32[]{:S(2)}) copy-start(bf16[1,2,1,448,1408]{4,3,2,1,0:T(8,128)(2,1)} %param.21) | copy-start | bytes 7569412
  11.5 41.3 %all-to-all-start = ((bf16[64,7,1024]{2,1,0:T(8,128)(2,1)}), bf16[64,7,1024]{2,1,0:T(8,128)(2,1)}, u32[]{:S(2)}, u32[]{:S(2)}) async-start(bf16[64,7,1024]{2,1,0:T(8,128)(2,1)} %reshape.486), calls=%async_computation | async-start | bytes 2097152 | tf_op jit(solution)/shard_map/all_to_all | solution.py:100
  55.3 34.6 %all-to-all-start.1 = ((bf16[64,7,1024]{2,1,0:T(8,128)(2,1)}), bf16[64,7,1024]{2,1,0:T(8,128)(2,1)}, u32[]{:S(2)}, u32[]{:S(2)}) async-start(bf16[64,7,1024]{2,1,0:T(8,128)(2,1)} %reshape.487), calls=%async_computation.1 | async-start | bytes 2097152 | tf_op jit(solution)/shard_map/all_to_all | solution.py:111
  98.8 8.1 %copy-start.18 = (f32[64,1024]{1,0:T(8,128)}, f32[64,1024]{1,0:T(8,128)S(1)}, u32[]{:S(2)}) copy-start(f32[64,1024]{1,0:T(8,128)S(1)} %reduce_sum.111) | copy-start | bytes 786436
  98.8 5.7 collective-permute-start
  114.1 35.8 %all-to-all-start.2 = ((bf16[64,7,1024]{2,1,0:T(8,128)(2,1)}), bf16[64,7,1024]{2,1,0:T(8,128)(2,1)}, u32[]{:S(2)}, u32[]{:S(2)}) async-start(bf16[64,7,1024]{2,1,0:T(8,128)(2,1)} %reshape.489), calls=%async_computation.2 | async-start | bytes 2097152 | tf_op jit(solution)/shard_map/all_to_all | solution.py:100
  152.5 34.7 %all-to-all-start.3 = ((bf16[64,7,1024]{2,1,0:T(8,128)(2,1)}), bf16[64,7,1024]{2,1,0:T(8,128)(2,1)}, u32[]{:S(2)}, u32[]{:S(2)}) async-start(bf16[64,7,1024]{2,1,0:T(8,128)(2,1)} %reshape.490), calls=%async_computation.3 | async-start | bytes 2097152 | tf_op jit(solution)/shard_map/all_to_all | solution.py:111
  193.8 10.6 %copy-start.15 = (bf16[2,64,1024]{2,1,0:T(8,128)(2,1)S(1)}, bf16[2,64,1024]{2,1,0:T(8,128)(2,1)}, u32[]{:S(2)}) copy-start(bf16[2,64,1024]{2,1,0:T(8,128)(2,1)} %param.17) | copy-start | bytes 786436
  198.5 98.7 %copy-start.5 = (bf16[2,64,1024]{2,1,0:T(8,128)(2,1)}, bf16[2,64,1024]{2,1,0:T(8,128)(2,1)S(1)}, u32[]{:S(2)}) copy-start(bf16[2,64,1024]{2,1,0:T(8,128)(2,1)S(1)} %get-tuple-element.172) | copy-start | bytes 786436
  198.5 5.9 %collective-permute-start.1 = (bf16[64,1024]{1,0:T(8,128)(2,1)}, bf16[64,1024]{1,0:T(8,128)(2,1)S(1)}, u32[]{:S(2)}, u32[]{:S(2)}) collective-permute-start(bf16[64,1024]{1,0:T(8,128)(2,1)} %get-tuple-element.173), channel_id=1, source_target_pairs={{64,0},{128,64},{192,128},{65,1},{129,65},{193,129},{66,2},{130,66... | collective-permute-start | bytes 393224 | tf_op jit(solution)/shard_map/ppermute | solution.py:10
  215.6 35.8 %all-to-all-start.4 = ((bf16[64,7,1024]{2,1,0:T(8,128)(2,1)}), bf16[64,7,1024]{2,1,0:T(8,128)(2,1)}, u32[]{:S(2)}, u32[]{:S(2)}) async-start(bf16[64,7,1024]{2,1,0:T(8,128)(2,1)} %reshape.492), calls=%async_computation.4 | async-start | bytes 2097152 | tf_op jit(solution)/shard_map/all_to_all | solution.py:100
  255.8 8.2 %copy-start.35 = (bf16[1,2,64,1024]{3,2,1,0:T(8,128)(2,1)S(1)}, bf16[1,2,64,1024]{3,2,1,0:T(8,128)(2,1)}, u32[]{:S(2)}) copy-start(bf16[1,2,64,1024]{3,2,1,0:T(8,128)(2,1)} %param.20) | copy-start | bytes 786436
  255.8 34.7 %all-to-all-start.5 = ((bf16[64,7,1024]{2,1,0:T(8,128)(2,1)}), bf16[64,7,1024]{2,1,0:T(8,128)(2,1)}, u32[]{:S(2)}, u32[]{:S(2)}) async-start(bf16[64,7,1024]{2,1,0:T(8,128)(2,1)} %reshape.493), calls=%async_computation.5 | async-start | bytes 2097152 | tf_op jit(solution)/shard_map/all_to_all | solution.py:111
  290.5 63.2 %all-to-all-start.10 = ((bf16[64,7,1024]{2,1,0:T(8,128)(2,1)}), bf16[64,7,1024]{2,1,0:T(8,128)(2,1)}, u32[]{:S(2)}, u32[]{:S(2)}) async-start(bf16[64,7,1024]{2,1,0:T(8,128)(2,1)} %reshape.502), calls=%async_computation.10 | async-start | bytes 2097152 | tf_op jit(solution)/shard_map/all_to_all | solution.py:137
  304.5 37.8 %copy-start.16 = (bf16[2,64,1024]{2,1,0:T(8,128)(2,1)S(1)}, bf16[2,64,1024]{2,1,0:T(8,128)(2,1)}, u32[]{:S(2)}) copy-start(bf16[2,64,1024]{2,1,0:T(8,128)(2,1)} %param.17) | copy-start | bytes 786436
  309.2 142.3 %copy-start.7 = (bf16[2,64,1024]{2,1,0:T(8,128)(2,1)}, bf16[2,64,1024]{2,1,0:T(8,128)(2,1)S(1)}, u32[]{:S(2)}) copy-start(bf16[2,64,1024]{2,1,0:T(8,128)(2,1)S(1)} %get-tuple-element.170) | copy-start | bytes 786436
  309.2 33.2 %collective-permute-start.2 = (bf16[64,1024]{1,0:T(8,128)(2,1)}, bf16[64,1024]{1,0:T(8,128)(2,1)S(1)}, u32[]{:S(2)}, u32[]{:S(2)}) collective-permute-start(bf16[64,1024]{1,0:T(8,128)(2,1)} %get-tuple-element.171), channel_id=1, source_target_pairs={{64,0},{128,64},{192,128},{65,1},{129,65},{193,129},{66,2},{130,66... | collective-permute-start | bytes 393224 | tf_op jit(solution)/shard_map/ppermute | solution.py:10
  353.7 12.1 %copy-start.31 = (bf16[64,1024]{1,0:T(8,128)(2,1)S(1)}, bf16[64,1024]{1,0:T(8,128)(2,1)}, u32[]{:S(2)}) copy-start(bf16[64,1024]{1,0:T(8,128)(2,1)} %get-tuple-element.186) | copy-start | bytes 393220
  353.7 39.2 %all-to-all-start.6 = ((bf16[64,7,1024]{2,1,0:T(8,128)(2,1)}), bf16[64,7,1024]{2,1,0:T(8,128)(2,1)}, u32[]{:S(2)}, u32[]{:S(2)}) async-start(bf16[64,7,1024]{2,1,0:T(8,128)(2,1)} %reshape.495), calls=%async_computation.6 | async-start | bytes 2097152 | tf_op jit(solution)/shard_map/all_to_all | solution.py:100
  392.9 34.7 %all-to-all-start.11 = ((bf16[64,7,1024]{2,1,0:T(8,128)(2,1)}), bf16[64,7,1024]{2,1,0:T(8,128)(2,1)}, u32[]{:S(2)}, u32[]{:S(2)}) async-start(bf16[64,7,1024]{2,1,0:T(8,128)(2,1)} %reshape.505), calls=%async_computation.11 | async-start | bytes 2097152 | tf_op jit(solution)/shard_map/all_to_all | solution.py:137
  427.6 34.5 %all-to-all-start.7 = ((bf16[64,7,1024]{2,1,0:T(8,128)(2,1)}), bf16[64,7,1024]{2,1,0:T(8,128)(2,1)}, u32[]{:S(2)}, u32[]{:S(2)}) async-start(bf16[64,7,1024]{2,1,0:T(8,128)(2,1)} %reshape.496), calls=%async_computation.7 | async-start | bytes 2097152 | tf_op jit(solution)/shard_map/all_to_all | solution.py:111
  471.2 5.8 %collective-permute-start.3 = (bf16[64,1024]{1,0:T(8,128)(2,1)S(1)}, bf16[64,1024]{1,0:T(8,128)(2,1)S(1)}, u32[]{:S(2)}, u32[]{:S(2)}) collective-permute-start(bf16[64,1024]{1,0:T(8,128)(2,1)S(1)} %get-tuple-element.169), channel_id=1, source_target_pairs={{64,0},{128,64},{192,128},{65,1},{129,65},{193,129},{66,2},{130,66... | collective-permute-start | bytes 393224 | tf_op jit(solution)/shard_map/ppermute | solution.py:10
  487.6 35.8 %all-to-all-start.8 = ((bf16[64,7,1024]{2,1,0:T(8,128)(2,1)}), bf16[64,7,1024]{2,1,0:T(8,128)(2,1)}, u32[]{:S(2)}, u32[]{:S(2)}) async-start(bf16[64,7,1024]{2,1,0:T(8,128)(2,1)} %reshape.498), calls=%async_computation.8 | async-start | bytes 2097152 | tf_op jit(solution)/shard_map/all_to_all | solution.py:100
  534.6 34.8 %all-to-all-start.9 = ((bf16[64,7,1024]{2,1,0:T(8,128)(2,1)}), bf16[64,7,1024]{2,1,0:T(8,128)(2,1)}, u32[]{:S(2)}, u32[]{:S(2)}) async-start(bf16[64,7,1024]{2,1,0:T(8,128)(2,1)} %reshape.499), calls=%async_computation.9 | async-start | bytes 2097152 | tf_op jit(solution)/shard_map/all_to_all | solution.py:111
  (31 other events, 85.6 us)
where the time goes:
time: 588 us; the launch traced here: 576 us
  waiting for transfers between devices  247 us (42%)
  local copies, waits for them, and re-layouts  140 us (24%)
  starting transfers between devices  102 us (17%)
  other arithmetic  59.9 us (10%)
  matrix products  26 us (4%)
    all_to_all x5, waiting for transfers between devices, per_device(): lax.all_to_all(outgoing, 'expert', split_axis=0, concat_axis=0, tiled=True)  109 us
    all_to_all x5, waiting for transfers between devices, per_device(): lax.all_to_all(row_grads.reshape(expert_count, capacity, model_width), 'e...  88.7 us
    all_to_all x5, starting transfers between devices, per_device(): lax.all_to_all(outgoing, 'expert', split_axis=0, concat_axis=0, tiled=True)  48.3 us
    ppermute x4, waiting for transfers between devices, shifted(): return lax.ppermute(value, axis, pairs)  40.6 us
    all_to_all x5, starting transfers between devices, per_device(): lax.all_to_all(row_grads.reshape(expert_count, capacity, model_width), 'e...  33.9 us
    dynamic_update_slice x14, other arithmetic, store_at(): lax.dynamic_update_index_in_dim(store, jnp.where(is_valid, value, previou...  24.4 us
    mul x15, local copies, waits for them, and re-layouts, per_device(): gate_now[:, :, None] * grad_in[:, None, :].astype(jnp.float32)  19.2 us
    scatter x5, other arithmetic, spread(): filled = jnp.zeros((expert_count * capacity, model_width), jnp.bfloat16)....  19 us
  transfers between devices with their start and end apart: 16, of which 15 were waited for; matrix products, arithmetic and copies ran while one was open for 22% of the time, Pallas kernels for 0%

commit v1 on v0

v1 whole, which is shorter than its diff:
```python
import functools

import jax
import jax.numpy as jnp
from jax import lax
from jax.experimental import pallas as pl
from jax.experimental.pallas import tpu as pltpu
from jax.sharding import PartitionSpec as P

MESH = pl.DeviceIdType.MESH
NZ = 8
PAD = 8
RIGHT, LEFT = 0, 1
F32, BF16 = jnp.float32, jnp.bfloat16


def block_of(direction, step):
    if step == 0:
        return 0
    if step == 4:
        return 7
    return 2 * step - 1 if direction == RIGHT else 2 * step


def streams(step):
    if step == 4:
        return ((0, RIGHT), (1, LEFT))
    return tuple((half, direction) for half in (0, 1) for direction in (RIGHT, LEFT))


def fused_kernel(
    dims,
    cot,
    smat,
    xin,
    saved_hbm,
    w1_hbm,
    w2_hbm,
    sec_out,
    g1_out,
    g2_out,
    gath,
    sendb,
    routed,
    rsend,
    rrecv,
    part,
    ring_send,
    ring_recv,
    gout,
    srecv,
    sel,
    comb,
    w1v,
    w2d,
    savedv,
    factor,
    act,
    fog,
    z_send,
    z_recv,
    y_send,
    y_recv,
    r_send,
    r_recv,
    q_send,
    q_recv,
    x_send,
    x_recv,
    s_send,
    s_recv,
    local_sem,
    own_sem,
):
    sections, nyc, tok, width, wide, cap = dims
    hidden = wide // 2
    half_cols = width // 2
    rows_in = NZ * nyc * cap
    rows = NZ * nyc * PAD
    per_peer = NZ * PAD
    pair_rows = 2 * nyc * PAD
    sel_rows = nyc * PAD

    pipe = lax.axis_index("pipe")
    expert = lax.axis_index("expert")
    zi = expert // nyc
    me = expert % nyc

    def along_z(by):
        return (pipe, ((zi + by) % NZ) * nyc + me)

    def along_y(yc):
        return (pipe, zi * nyc + yc)

    right, left = along_z(1), along_z(NZ - 1)
    x_next = ((pipe + sections - 1) % sections, expert)
    x_prev = ((pipe + 1) % sections, expert)

    weight_copies = (
        pltpu.make_async_copy(w1_hbm, w1v, local_sem.at[0]),
        pltpu.make_async_copy(w2_hbm, w2d.at[pl.ds(0, hidden), :], local_sem.at[1]),
        pltpu.make_async_copy(w2_hbm, w2d.at[pl.ds(hidden, hidden), :], local_sem.at[2]),
        pltpu.make_async_copy(saved_hbm.at[0], savedv.at[0, pl.ds(0, rows_in), :], local_sem.at[3]),
        pltpu.make_async_copy(saved_hbm.at[1], savedv.at[1, pl.ds(0, rows_in), :], local_sem.at[4]),
    )

    barrier = pltpu.get_barrier_semaphore()
    for by in range(1, NZ):
        pl.semaphore_signal(barrier, inc=1, device_id=along_z(by), device_id_type=MESH)
    for by in range(1, nyc):
        pl.semaphore_signal(
            barrier, inc=1, device_id=along_y((me + by) % nyc), device_id_type=MESH
        )
    pl.semaphore_signal(barrier, inc=1, device_id=x_next, device_id_type=MESH)
    pl.semaphore_signal(barrier, inc=1, device_id=x_prev, device_id_type=MESH)

    for copy in weight_copies:
        copy.start()
    for mb in range(2):
        gath[2 + mb, 0, 0:tok, :] = xin[mb]
        if rows > rows_in:
            savedv[mb, rows_in:rows, :] = jnp.zeros((rows - rows_in, wide), BF16)

    @pl.when(pipe == sections - 1)
    def _():
        for mb in range(2):
            gath[mb, 0, 0:tok, :] = cot[mb]

    srecv[0] = smat[pl.ds(pl.multiple_of(zi * sel_rows, sel_rows), sel_rows), :]
    pl.semaphore_wait(barrier, NZ + nyc)

    def selection_copy(by):
        at = 2 * by - 1 if by <= 4 else 2 * (NZ - by)
        to = (zi + by) % NZ
        return pltpu.make_async_remote_copy(
            src_ref=smat.at[pl.ds(pl.multiple_of(to * sel_rows, sel_rows), sel_rows), :],
            dst_ref=srecv.at[at],
            send_sem=s_send.at[by],
            recv_sem=s_recv.at[at],
            device_id=along_z(by),
            device_id_type=MESH,
        )

    def block_view(task, at, half):
        return gath.at[
            task, at // 2, pl.ds((at % 2) * tok, tok), pl.ds(half * half_cols, half_cols)
        ]

    def z_copy(task, direction, step, half):
        return pltpu.make_async_remote_copy(
            src_ref=block_view(task, block_of(direction, step - 1), half),
            dst_ref=block_view(task, block_of(direction, step), half),
            send_sem=z_send.at[task, direction, step - 1, half],
            recv_sem=z_recv.at[task, direction, step - 1, half],
            device_id=right if direction == RIGHT else left,
            device_id_type=MESH,
        )

    def y_copy(task, by, at, count):
        to = (me + by) % nyc
        return pltpu.make_async_remote_copy(
            src_ref=sendb.at[task, to, pl.ds(at, count), :],
            dst_ref=routed.at[task, me, pl.ds(at, count), :],
            send_sem=y_send.at[task, by],
            recv_sem=y_recv.at[task, by],
            device_id=along_y(to),
            device_id_type=MESH,
        )

    def y_arrival(task, by):
        of = (me + nyc - by) % nyc
        return pltpu.make_async_remote_copy(
            src_ref=sendb.at[task, of],
            dst_ref=routed.at[task, of],
            send_sem=y_send.at[task, by],
            recv_sem=y_recv.at[task, by],
            device_id=along_y(of),
            device_id_type=MESH,
        )

    def own_copy(task):
        return pltpu.make_async_copy(sendb.at[task, me], routed.at[task, me], own_sem.at[task])

    def r_copy(mb, by):
        to = (me + by) % nyc
        return pltpu.make_async_remote_copy(
            src_ref=rsend.at[mb, to],
            dst_ref=rrecv.at[mb, me],
            send_sem=r_send.at[mb, by],
            recv_sem=r_recv.at[mb, by],
            device_id=along_y(to),
            device_id_type=MESH,
        )

    def r_arrival(mb, by):
        of = (me + nyc - by) % nyc
        return pltpu.make_async_remote_copy(
            src_ref=rsend.at[mb, of],
            dst_ref=rrecv.at[mb, of],
            send_sem=r_send.at[mb, by],
            recv_sem=r_recv.at[mb, by],
            device_id=along_y(of),
            device_id_type=MESH,
        )

    def own_return(mb):
        return pltpu.make_async_copy(rsend.at[mb, me], rrecv.at[mb, me], own_sem.at[4 + mb])

    def q_copy(mb, direction, step, half):
        cols = pl.ds(half * half_cols, half_cols)
        return pltpu.make_async_remote_copy(
            src_ref=ring_send.at[mb, direction, step - 1, :, cols],
            dst_ref=ring_recv.at[mb, direction, step - 1, :, cols],
            send_sem=q_send.at[mb, direction, step - 1, half],
            recv_sem=q_recv.at[mb, direction, step - 1, half],
            device_id=right if direction == RIGHT else left,
            device_id_type=MESH,
        )

    def x_copy(mb, half):
        return pltpu.make_async_remote_copy(
            src_ref=gout.at[mb, :, pl.ds(half * half_cols, half_cols)],
            dst_ref=block_view(mb, 0, half),
            send_sem=x_send.at[mb, half],
            recv_sem=x_recv.at[mb, half],
            device_id=x_next,
            device_id_type=MESH,
        )

    def plan(turn):
        mb = turn - (sections - 1 - pipe)
        is_grad = (mb >= 0) & (mb < 2)
        last = pipe == sections - 1
        before = pipe == sections - 2
        x_turn = jnp.where(last, turn - 2, jnp.where(before, jnp.where(turn == 0, 0, turn - 2), turn))
        is_x = jnp.logical_not(is_grad) & (x_turn >= 0) & (x_turn < 2)
        task = jnp.where(is_grad, mb, 2 + x_turn)
        return mb, is_grad, is_grad | is_x, task

    def ring_start(task):
        for half, direction in streams(1):
            z_copy(task, direction, 1, half).start()

    for by in range(1, NZ):
        selection_copy(by).start()
    ring_start(plan(0)[3])

    lane = lax.broadcasted_iota(jnp.int32, (sel_rows, 2 * tok), 1)
    low = lane < tok
    for by in range(1, NZ):
        selection_copy(by).wait_recv()
    for pair in range(NZ // 2):
        first, second = srecv[2 * pair].astype(F32), srecv[2 * pair + 1].astype(F32)
        for mb in range(2):
            one = first if mb == 0 else pltpu.roll(first, tok, 1)
            two = second if mb == 1 else pltpu.roll(second, tok, 1)
            one = jnp.where(low, one, 0.0)
            two = jnp.where(low, 0.0, two)
            pieces = []
            for yc in range(nyc):
                pieces += [one[yc * PAD : (yc + 1) * PAD], two[yc * PAD : (yc + 1) * PAD]]
            both = jnp.concatenate(pieces, axis=0)
            ones = jnp.where(both != 0.0, 1.0, 0.0)
            sel[mb, pair] = both.astype(BF16)
            sel[2 + mb, pair] = ones.astype(BF16)
            comb[mb, pair] = ones.T.astype(BF16)

    def gather(task):
        for step in range(1, 5):
            for half, direction in streams(step):
                z_copy(task, direction, step, half).wait_recv()
                if step < 4 and (half, direction) in streams(step + 1):
                    z_copy(task, direction, step + 1, half).start()
            pair = step - 1
            chosen = jnp.dot(sel[task, pair], gath[task, pair], preferred_element_type=F32).astype(
                BF16
            )
            at = pair * 2 * PAD
            for yc in range(nyc):
                sendb[task, yc, at : at + 2 * PAD, :] = chosen[
                    yc * 2 * PAD : (yc + 1) * 2 * PAD
                ]
            for by in range(1, nyc):
                y_copy(task, by, at, 2 * PAD).start()
        own_copy(task).start()

    def finish_gather(task):
        for by in range(1, nyc):
            y_arrival(task, by).wait_recv()
        own_copy(task).wait()

    def finish_sends(task):
        for step in range(1, 5):
            for half, direction in streams(step):
                z_copy(task, direction, step, half).wait_send()
        for by in range(1, nyc):
            y_arrival(task, by).wait_send()

    chunk = min(128, rows)

    def factors(mb):
        def body(i, carry):
            at = pl.multiple_of(i * chunk, chunk)
            row = lax.broadcasted_iota(jnp.int32, (chunk, rows), 0) + at
            col = lax.broadcasted_iota(jnp.int32, (chunk, rows), 1)
            yc = row // per_peer
            block = (row // PAD) % NZ
            slot = row % PAD
            rel = jnp.where(block % 2 == 1, NZ - (block + 1) // 2, block // 2)
            zz = (zi + rel) % NZ
            want = zz * (nyc * cap) + yc * cap + slot
            pick = jnp.where((col == want) & (slot < cap), 1.0, 0.0).astype(BF16)
            val = jnp.dot(pick, savedv[mb], preferred_element_type=F32)
            swapped = pltpu.roll(val, hidden, 1)
            is_gate = lax.broadcasted_iota(jnp.int32, (chunk, wide), 1) < hidden
            a = jnp.where(is_gate, val, swapped)
            u = jnp.where(is_gate, swapped, val)
            sg = jax.nn.sigmoid(a)
            silu = a * sg
            factor[mb, pl.ds(at, chunk), :] = jnp.where(
                is_gate, u * (sg * (1.0 + a * (1.0 - sg))), silu
            )
            act[pl.ds(mb * rows + at, chunk), :] = (silu * u)[:, : act.shape[1]].astype(BF16)
            return carry

        lax.fori_loop(0, rows // chunk, body, 0)

    def expert_stage(mb):
        block = min(256, rows)
        peers = block // per_peer

        def body(i, carry):
            at = pl.multiple_of(i * block, block)
            incoming = routed[mb, pl.ds(i * peers, peers)].reshape(block, width)
            grad = lax.dot_general(
                incoming, w2d[...], (((1,), (1,)), ((), ())), preferred_element_type=F32
            )
            out = (grad * factor[mb, pl.ds(at, block), :]).astype(BF16)
            fog[mb, pl.ds(at, block), :] = out
            back = lax.dot_general(
                out, w1v[...], (((1,), (1,)), ((), ())), preferred_element_type=F32
            ).astype(BF16)
            rsend[mb, pl.ds(i * peers, peers)] = back.reshape(peers, per_peer, width)
            return carry

        lax.fori_loop(0, rows // block, body, 0)
        for by in range(1, nyc):
            r_copy(mb, by).start()
        own_return(mb).start()

    def combine(mb):
        for by in range(1, nyc):
            r_arrival(mb, by).wait_recv()
        own_return(mb).wait()

        def partial_sums(pair):
            back = jnp.concatenate(
                [rrecv[mb, yc, pair * 2 * PAD : (pair + 1) * 2 * PAD, :] for yc in range(nyc)],
                axis=0,
            )
            part[pair] = jnp.dot(comb[mb, pair], back, preferred_element_type=F32)

        def partial_of(at, half):
            return part[
                at // 2,
                (at % 2) * tok : (at % 2 + 1) * tok,
                half * half_cols : (half + 1) * half_cols,
            ]

        def send(direction, step, half, value):
            ring_send[
                mb, direction, step - 1, :, half * half_cols : (half + 1) * half_cols
            ] = value.astype(BF16)
            q_copy(mb, direction, step, half).start()

        def received(direction, step, half):
            q_copy(mb, direction, step, half).wait_recv()
            return ring_recv[
                mb, direction, step - 1, :, half * half_cols : (half + 1) * half_cols
            ].astype(F32)

        partial_sums(3)
        send(RIGHT, 1, 0, partial_of(7, 0))
        send(LEFT, 1, 1, partial_of(7, 1))
        partial_sums(2)
        send(RIGHT, 2, 1, partial_of(6, 1))
        send(LEFT, 2, 0, partial_of(5, 0))
        partial_sums(1)
        partial_sums(0)
        send(RIGHT, 2, 0, partial_of(6, 0) + received(RIGHT, 1, 0))
        send(LEFT, 2, 1, partial_of(5, 1) + received(LEFT, 1, 1))
        for step in (3, 4):
            for half in ((1, 0) if step == 3 else (1, 0)):
                for direction in (RIGHT, LEFT):
                    at = block_of(LEFT if direction == RIGHT else RIGHT, 5 - step)
                    send(
                        direction,
                        step,
                        half,
                        partial_of(at, half) + received(direction, step - 1, half),
                    )
        for half in (1, 0):
            cols = slice(half * half_cols, (half + 1) * half_cols)
            total = gath[mb, 0, 0:tok, cols].astype(F32) + partial_of(0, half)
            total = total + received(RIGHT, 4, half) + received(LEFT, 4, half)
            gout[mb, :, cols] = total.astype(BF16)

            @pl.when(pipe > 0)
            def _():
                x_copy(mb, half).start()

        sec_out[mb] = gout[mb]

    def finish_return(mb):
        for by in range(1, nyc):
            r_arrival(mb, by).wait_send()
        for half, direction in streams(4):
            q_copy(mb, direction, 1, half).wait_send()
        for step in range(2, 5):
            for half, direction in streams(1):
                q_copy(mb, direction, step, half).wait_send()

        @pl.when(pipe > 0)
        def _():
            for half in range(2):
                x_copy(mb, half).wait_send()

    def turn_body(turn, carry):
        mb, is_grad, is_any, task = plan(turn)

        @pl.when(is_any)
        def _():
            @pl.when(is_grad & (pipe < sections - 1))
            def _():
                for half in (1, 0):
                    x_copy(mb, half).wait_recv()

            @pl.when(turn > 0)
            def _():
                ring_start(task)

            gather(task)

        @pl.when(turn == 0)
        def _():
            for copy in weight_copies:
                copy.wait()

        @pl.when(turn < 2)
        def _():
            factors(turn)

        @pl.when(is_any)
        def _():
            finish_gather(task)

        @pl.when(is_grad)
        def _():
            expert_stage(mb)
            combine(mb)
            finish_return(mb)

        @pl.when(is_any)
        def _():
            finish_sends(task)

        return carry

    lax.fori_loop(0, sections + 1, turn_body, 0)
    for by in range(1, NZ):
        selection_copy(by).wait_send()

    both_rows = 2 * rows
    tile = 256
    grads = routed[0:2].reshape(both_rows, width)
    for start in range(0, hidden, tile):
        stop = min(start + tile, hidden)
        lanes = act[:, start : min(start + tile, act.shape[1])]
        g2 = lax.dot_general(lanes, grads, (((0,), (0,)), ((), ())), preferred_element_type=F32)
        g2_out[start:stop, :] = g2[: stop - start].astype(BF16)
    outs = fog[...].reshape(both_rows, wide)

    def g1_body(i, carry):
        at = pl.multiple_of(i * tile, tile)
        lanes = routed[2:4, :, :, pl.ds(at, tile)].reshape(both_rows, tile)
        g1 = lax.dot_general(lanes, outs, (((0,), (0,)), ((), ())), preferred_element_type=F32)
        g1_out[pl.ds(at, tile), :] = g1.astype(BF16)
        return carry

    lax.fori_loop(0, width // tile, g1_body, 0)


def selection(ids, gates, experts):
    micro, tok, top = ids.shape
    flat = ids.reshape(micro, tok * top)
    order = jnp.arange(tok * top)
    earlier = (flat[:, :, None] == flat[:, None, :]) & (order[None, :] < order[:, None])[None]
    slot = jnp.sum(earlier.astype(jnp.int32), axis=2)
    target = (flat * PAD + slot).reshape(micro * tok, top)
    row = lax.broadcasted_iota(jnp.int32, (experts * PAD, micro * tok), 0)
    weight = gates.reshape(micro * tok, top)
    out = jnp.zeros((experts * PAD, micro * tok), F32)
    for k in range(top):
        out = out + jnp.where(row == target[None, :, k], weight[None, :, k], 0.0)
    return out.astype(BF16)


def per_device(cotangent, expert_ids, gates, layer_inputs, saved_fc1, w_fc1, w_fc2):
    experts = lax.axis_size("expert")
    sections = lax.axis_size("pipe")
    nyc = experts // NZ
    micro, tok, width = cotangent.shape
    slots, wide = saved_fc1.shape[3:]
    hidden = wide // 2
    cap = slots // experts
    rows = experts * PAD
    per_peer = NZ * PAD
    smat = selection(expert_ids[0], gates[0], experts)
    dims = (sections, nyc, tok, width, wide, cap)
    vmem = pl.BlockSpec(memory_space=pltpu.VMEM)
    hbm = pl.BlockSpec(memory_space=pl.ANY)
    act_width = -(-hidden // 256) * 256
    dma = pltpu.SemaphoreType.DMA
    out = pl.pallas_call(
        functools.partial(fused_kernel, dims),
        out_shape=(
            jax.ShapeDtypeStruct((micro, tok, width), BF16),
            jax.ShapeDtypeStruct((width, wide), BF16),
            jax.ShapeDtypeStruct((hidden, width), BF16),
        ),
        in_specs=[vmem, vmem, vmem, hbm, hbm, hbm],
        out_specs=(vmem, vmem, vmem),
        scratch_shapes=[
            pltpu.VMEM((4, NZ // 2, 2 * tok, width), BF16),
            pltpu.VMEM((4, nyc, per_peer, width), BF16),
            pltpu.VMEM((4, nyc, per_peer, width), BF16),
            pltpu.VMEM((2, nyc, per_peer, width), BF16),
            pltpu.VMEM((2, nyc, per_peer, width), BF16),
            pltpu.VMEM((NZ // 2, 2 * tok, width), F32),
            pltpu.VMEM((2, 2, 4, tok, width), BF16),
            pltpu.VMEM((2, 2, 4, tok, width), BF16),
            pltpu.VMEM((2, tok, width), BF16),
            pltpu.VMEM((NZ, nyc * PAD, 2 * tok), BF16),
            pltpu.VMEM((4, NZ // 2, 2 * nyc * PAD, 2 * tok), BF16),
            pltpu.VMEM((2, NZ // 2, 2 * tok, 2 * nyc * PAD), BF16),
            pltpu.VMEM((width, wide), BF16),
            pltpu.VMEM((wide, width), BF16),
            pltpu.VMEM((2, rows, wide), BF16),
            pltpu.VMEM((2, rows, wide), F32),
            pltpu.VMEM((2 * rows, act_width), BF16),
            pltpu.VMEM((2, rows, wide), BF16),
            dma((4, 2, 4, 2)),
            dma((4, 2, 4, 2)),
            dma((4, nyc)),
            dma((4, nyc)),
            dma((2, nyc)),
            dma((2, nyc)),
            dma((2, 2, 4, 2)),
            dma((2, 2, 4, 2)),
            dma((2, 2)),
            dma((2, 2)),
            dma((NZ,)),
            dma((NZ,)),
            dma((5,)),
            dma((6,)),
        ],
        compiler_params=pltpu.CompilerParams(
            collective_id=0, has_side_effects=True, vmem_limit_bytes=60 * 1024 * 1024
        ),
        name="split_backward",
    )(cotangent, smat, layer_inputs[0], saved_fc1[0, :, 0], w_fc1[0, 0], w_fc2[0, 0])
    return out[0][None], out[1][None, None], out[2][None, None]


def solution(mesh):
    in_specs = (
        P(None, "expert", None),
        P("pipe", None, "expert", None),
        P("pipe", None, "expert", None),
        P("pipe", None, "expert", None),
        P("pipe", None, "expert", None, None),
        P("pipe", "expert", None, None),
        P("pipe", "expert", None, None),
    )
    out_specs = (
        P("pipe", None, "expert", None),
        P("pipe", "expert", None, None),
        P("pipe", "expert", None, None),
    )
    return jax.shard_map(
        per_device, mesh=mesh, in_specs=in_specs, out_specs=out_specs, check_vma=False
    )
```

time: 588 us -> 314 us (0.53); the launches traced: 576 us -> 314 us
  Pallas kernels: 0 us -> 303 us
  waiting for transfers between devices: 247 us -> 0 us
  local copies, waits for them, and re-layouts: 140 us -> 8.75 us
  starting transfers between devices: 102 us -> 0 us
  other arithmetic: 59.9 us -> 2.01 us
  matrix products: 26 us -> 0 us
    pallas_call x0 -> x1, Pallas kernels: none -> 303 us  [per_device(): pl.pallas_call(functools.partial(fused_kernel, dims), out_shape=(jax.Shap...]
    all_to_all x12 -> x0, waiting for transfers between devices: 206 us -> none  [the longest x5 109 us: per_device(): lax.all_to_all(outgoing, 'expert', split_axis=0, concat_axis=0, tiled=True)]
    all_to_all x12 -> x0, starting transfers between devices: 95.5 us -> none  [the longest x5 48.3 us: per_device(): lax.all_to_all(outgoing, 'expert', split_axis=0, concat_axis=0, tiled=True)]
    reshape x27 -> x0, local copies, waits for them, and re-layouts: 50.7 us -> none  [the longest x7 13.7 us: spread(): return filled.reshape(expert_count, capacity, model_width)]
    ppermute x4 -> x0, waiting for transfers between devices: 40.6 us -> none  [shifted(): return lax.ppermute(value, axis, pairs)]
    dot_general x15 -> x0, matrix products: 26 us -> none  [the longest x2 6.76 us: expert_grads(): lax.dot_general(fc1_out_grad, weight_one, (((1,), (1,)), ((), ())), prefe...]
    dynamic_update_slice x14 -> x0, other arithmetic: 24.4 us -> none  [store_at(): lax.dynamic_update_index_in_dim(store, jnp.where(is_valid, value, previou...]
    mul x29 -> x1, local copies, waits for them, and re-layouts: 20.8 us -> 0.1 us  [selection(): target = (flat * PAD + slot).reshape(micro * tok, top)]
  transfers between devices with their start and end apart: 16 -> 0, of which waited for: 15 -> 0; matrix products, arithmetic and copies ran while one was open for 22% -> 0% of each run, Pallas kernels for 0% -> 0%
where the time goes in v1:
time: 314 us
  Pallas kernels  303 us (96%)
  local copies, waits for them, and re-layouts  8.75 us (3%)
    pallas_call x1, Pallas kernels, per_device(): pl.pallas_call(functools.partial(fused_kernel, dims), out_shape=(jax.Shap...  303 us
    unnamed x6, local copies, waits for them, and re-layouts  7.28 us

profile of v1, /device:TPU:1, one launch (start us, length us, event | category | flops | bytes accessed | tf_op | source)
XLA Modules:
  0.0 314.2 jit_solution(1905085419272909743)
XLA Ops:
  0.6 0.8 reshape_squeeze.4
  1.4 0.7 broadcast_multiply_fusion
  2.1 0.1 copy.14
  2.2 0.8 copy.15
  3.0 0.1 eq.75
  3.2 0.4 convert_reduce_fusion
  3.6 0.1 reduce_sum.12
  3.8 0.3 slice_reduce_fusion.5
  4.1 0.8 add_convert_fusion.smat
  4.9 302.7 %split_backward.1 = (bf16[2,64,1024]{2,1,0:T(8,128)(2,1)}, bf16[1024,1408]{1,0:T(8,128)(2,1)}, bf16[704,1024]{1,0:T(8,128)(2,1)}) custom-call(bf16[2,64,1024]{2,1,0:T(8,128)(2,1)} %cot.1, bf16[512,128]{1,0:T(8,128)(2,1)} %add_convert_fusion.smat, bf16[2,64,1024]{2,1,0:T(8,128)(2,1)} %bitcast.29, bf16[2,448,1408]{2,1,0:T(8,128)(2,1)} %bitcast.26, ...), custom_call_target="tpu_custom_call" | custom-call | tf_op jit(solution)/shard_map/split_backward/pallas_call | solution.py:524
  307.7 1.7 copy.19
  309.4 0.0 copy-start
  309.4 3.7 %copy.20 = bf16[1,1,1024,1408]{3,2,1,0:T(8,128)(2,1)} copy(bf16[1,1,1024,1408]{3,2,1,0:T(8,128)(2,1)} %bitcast.25) | data formatting | bytes 5767168
  313.1 0.0 copy-done
  313.1 1.1 copy.21
  (3 shorter events, 0.1 us)
Async XLA Ops:
  309.4 3.7 %copy-start = (bf16[704,1024]{1,0:T(8,128)(2,1)S(1)}, bf16[704,1024]{1,0:T(8,128)(2,1)}, u32[]{:S(2)}) copy-start(bf16[704,1024]{1,0:T(8,128)(2,1)} %get-tuple-element.8) | copy-start | bytes 4325380

commit v2 on v1

v2 whole, which is shorter than its diff:
```python
import functools

import jax
import jax.numpy as jnp
from jax import lax
from jax.experimental import pallas as pl
from jax.experimental.pallas import tpu as pltpu
from jax.sharding import PartitionSpec as P

MESH = pl.DeviceIdType.MESH
NZ = 8
PAD = 8
F32, BF16 = jnp.float32, jnp.bfloat16


SUMS = {
    0: (1, (0, 1), 6),
    1: (2, (0,), 7),
    2: (-1, (0, 1), 5),
    3: (-2, (1,), 7),
    4: (2, (0, 1), 4),
    5: (-2, (0, 1), 3),
    6: (1, (0, 1), 2),
    7: (-1, (0, 1), 1),
}


def fused_kernel(
    dims,
    cot,
    smat,
    xin,
    saved_hbm,
    w1_hbm,
    w2_hbm,
    sec_out,
    g1_out,
    g2_out,
    gath,
    sendb,
    routed,
    rsend,
    rrecv,
    part,
    sum_send,
    sum_recv,
    gout,
    srecv,
    sel,
    comb,
    w1v,
    w2d,
    savedv,
    factor,
    act,
    fog,
    d_send,
    e_send,
    f_send,
    z_recv,
    y_send,
    y_recv,
    r_send,
    r_recv,
    q_send,
    q_recv,
    s_send,
    s_recv,
    local_sem,
):
    sections, nyc, tok, width, wide, cap = dims
    hidden = wide // 2
    half_cols = width // 2
    rows_in = NZ * nyc * cap
    rows = NZ * nyc * PAD
    per_peer = NZ * PAD
    pair_rows = 2 * nyc * PAD
    sel_rows = nyc * PAD
    group = nyc // 2

    pipe = lax.axis_index("pipe")
    expert = lax.axis_index("expert")
    zi = expert // nyc
    me = expert % nyc
    core = me % 2
    place = core * group + me // 2

    def along_z(by, plane=None):
        return (pipe if plane is None else plane, ((zi + by + NZ) % NZ) * nyc + me)

    def along_y(yc):
        return (pipe, zi * nyc + yc)

    is_last = pipe == sections - 1
    before = (pipe + sections - 1) % sections
    after = (pipe + 1) % sections

    weight_copies = (
        pltpu.make_async_copy(w1_hbm, w1v, local_sem.at[0]),
        pltpu.make_async_copy(w2_hbm, w2d.at[pl.ds(0, hidden), :], local_sem.at[1]),
        pltpu.make_async_copy(w2_hbm, w2d.at[pl.ds(hidden, hidden), :], local_sem.at[2]),
        pltpu.make_async_copy(saved_hbm.at[0], savedv.at[0, pl.ds(0, rows_in), :], local_sem.at[3]),
        pltpu.make_async_copy(saved_hbm.at[1], savedv.at[1, pl.ds(0, rows_in), :], local_sem.at[4]),
    )

    barrier = pltpu.get_barrier_semaphore()
    for by in range(1, NZ):
        pl.semaphore_signal(barrier, inc=1, device_id=along_z(by), device_id_type=MESH)
    for by in range(1, nyc):
        pl.semaphore_signal(
            barrier, inc=1, device_id=along_y((me + by) % nyc), device_id_type=MESH
        )
    for by in range(-2, 3):
        for plane in (before, after):
            pl.semaphore_signal(
                barrier, inc=1, device_id=along_z(by, plane), device_id_type=MESH
            )

    for copy in weight_copies:
        copy.start()
    for mb in range(2):
        gath[2 + mb, 0, 0:tok, :] = xin[mb]
        if rows > rows_in:
            savedv[mb, rows_in:rows, :] = jnp.zeros((rows - rows_in, wide), BF16)

    @pl.when(is_last)
    def _():
        for mb in range(2):
            gath[mb, 0, 0:tok, :] = cot[mb]

    srecv[0] = smat[pl.ds(pl.multiple_of(zi * sel_rows, sel_rows), sel_rows), :]
    pl.semaphore_wait(barrier, NZ + nyc - 2 + 10)

    def selection_copy(by):
        at = 2 * by - 1 if by <= 4 else 2 * (NZ - by)
        to = (zi + by) % NZ
        return pltpu.make_async_remote_copy(
            src_ref=smat.at[pl.ds(pl.multiple_of(to * sel_rows, sel_rows), sel_rows), :],
            dst_ref=srecv.at[at],
            send_sem=s_send.at[by],
            recv_sem=s_recv.at[at],
            device_id=along_z(by),
            device_id_type=MESH,
        )

    def block_view(task, at, half):
        return gath.at[
            task, at // 2, pl.ds((at % 2) * tok, tok), pl.ds(half * half_cols, half_cols)
        ]

    def spread_copy(src, task, by, at, half, sem, plane=None):
        return pltpu.make_async_remote_copy(
            src_ref=src,
            dst_ref=block_view(task, at, half),
            send_sem=sem,
            recv_sem=z_recv.at[task, at, half],
            device_id=along_z(by, plane),
            device_id_type=MESH,
        )

    def spread_own(task):
        for by, at in ((2, 3), (-2, 4), (1, 1), (-1, 2)):
            for half in range(2):
                src = block_view(task, 0, half)
                spread_copy(src, task, by, at, half, d_send.at[task]).start()

    def spread_on(mb):
        for by, at in ((2, 3), (-2, 4), (1, 1), (-1, 2), (0, 0)):
            for half in range(2):
                src = gout.at[mb, :, pl.ds(half * half_cols, half_cols)]
                spread_copy(src, mb, by, at, half, e_send.at[mb], before).start()

    def wait_block(task, at, half):
        wait_for(block_view(task, at, half), z_recv.at[task, at, half])

    def y_copy(task, by, at, count):
        to = (me + by) % nyc
        return pltpu.make_async_remote_copy(
            src_ref=sendb.at[task, to, pl.ds(at, count), :],
            dst_ref=routed.at[task, place, pl.ds(at, count), :],
            send_sem=y_send.at[task],
            recv_sem=y_recv.at[task, core],
            device_id=along_y(to),
            device_id_type=MESH,
        )

    def own_copy(task):
        return pltpu.make_async_copy(
            sendb.at[task, me], routed.at[task, place], y_recv.at[task, core]
        )

    def wait_for(ref, sem):
        pltpu.make_async_copy(ref, ref, sem).wait()

    def wait_rows(task, of_core):
        wait_for(
            routed.at[task, pl.ds(of_core * group, group)], y_recv.at[task, of_core]
        )

    def r_copy(mb, pair, to):
        at = (to % 2) * group + to // 2
        return pltpu.make_async_remote_copy(
            src_ref=rsend.at[mb, at, pl.ds(pair * 2 * PAD, 2 * PAD), :],
            dst_ref=rrecv.at[mb, pair, me],
            send_sem=r_send.at[mb, to % 2],
            recv_sem=r_recv.at[mb, pair],
            device_id=along_y(to),
            device_id_type=MESH,
        )

    def own_return(mb, pair):
        return pltpu.make_async_copy(
            rsend.at[mb, place, pl.ds(pair * 2 * PAD, 2 * PAD), :],
            rrecv.at[mb, pair, me],
            r_recv.at[mb, pair],
        )

    def q_copy(mb, slot, half):
        cols = pl.ds(half * half_cols, half_cols)
        return pltpu.make_async_remote_copy(
            src_ref=sum_send.at[mb, slot, :, cols],
            dst_ref=sum_recv.at[mb, slot, :, cols],
            send_sem=q_send.at[mb],
            recv_sem=q_recv.at[mb, slot],
            device_id=along_z(SUMS[slot][0]),
            device_id_type=MESH,
        )

    def plan(turn):
        chunk_no = turn - 2
        is_chunk = (turn >= 2) & (turn < 6)
        mb, of_core = (turn - 2) // 2, turn % 2
        is_own = is_chunk & (of_core == core)
        is_x = ((turn < 2) & jnp.logical_not(is_last)) | ((turn >= 6) & is_last)
        task = jnp.where(is_chunk, mb, 2 + turn % 2)
        is_done = (turn >= 3) & (turn <= 6) & (of_core != core)
        is_done = is_done & jnp.logical_not((turn == 6) & (pipe == 0))
        return mb, of_core, is_chunk, is_own, is_own | is_x, task, is_done, (chunk_no - 1) // 2

    @pl.when(is_last & (core == 0))
    def _():
        spread_own(0)

    for by in range(1, NZ):
        selection_copy(by).start()

    @pl.when(jnp.logical_not(is_last))
    def _():
        spread_own(2)
        spread_own(3)

    lane = lax.broadcasted_iota(jnp.int32, (sel_rows, 2 * tok), 1)
    low = lane < tok
    for by in range(1, NZ):
        selection_copy(by).wait_recv()
    for pair in range(NZ // 2):
        first, second = srecv[2 * pair].astype(F32), srecv[2 * pair + 1].astype(F32)
        for mb in range(2):
            one = first if mb == 0 else pltpu.roll(first, tok, 1)
            two = second if mb == 1 else pltpu.roll(second, tok, 1)
            one = jnp.where(low, one, 0.0)
            two = jnp.where(low, 0.0, two)
            pieces = []
            for yc in range(nyc):
                pieces += [one[yc * PAD : (yc + 1) * PAD], two[yc * PAD : (yc + 1) * PAD]]
            both = jnp.concatenate(pieces, axis=0)
            ones = jnp.where(both != 0.0, 1.0, 0.0)
            sel[mb, pair] = both.astype(BF16)
            sel[2 + mb, pair] = ones.astype(BF16)
            comb[mb, pair] = ones.T.astype(BF16)

    @pl.when(is_last & (core == 1))
    def _():
        spread_own(0)

    def select(task, pair):
        chosen = jnp.dot(sel[task, pair], gath[task, pair], preferred_element_type=F32).astype(BF16)
        at = pair * 2 * PAD
        for yc in range(nyc):
            sendb[task, yc, at : at + 2 * PAD, :] = chosen[yc * 2 * PAD : (yc + 1) * 2 * PAD]
        for by in range(1, nyc):
            y_copy(task, by, at, 2 * PAD).start()

    def gather(task, is_handed_on):
        def forward(from_at, by, at, half):
            src = block_view(task, from_at, half)
            spread_copy(src, task, by, at, half, f_send.at[task]).start()

        wait_block(task, 3, 0)
        forward(3, 2, 7, 0)
        forward(3, 1, 5, 0)
        wait_block(task, 4, 1)
        forward(4, -2, 7, 1)
        forward(4, -1, 6, 1)
        wait_block(task, 3, 1)
        forward(3, 1, 5, 1)
        wait_block(task, 4, 0)
        forward(4, -1, 6, 0)
        for half in range(2):
            wait_block(task, 1, half)

        @pl.when(is_handed_on)
        def _():
            for half in range(2):
                wait_block(task, 0, half)

        select(task, 0)
        for pair, needs in ((1, (2,)), (2, (5,)), (3, (6, 7))):
            for at in needs:
                for half in range(2):
                    wait_block(task, at, half)
            select(task, pair)
        own_copy(task).start()

    chunk = min(128, rows)

    half_rows = rows // 2

    def factors(mb, of_core):
        def body(i, carry):
            at = pl.multiple_of(of_core * half_rows + i * chunk, chunk)
            row = lax.broadcasted_iota(jnp.int32, (chunk, rows), 0) + at
            col = lax.broadcasted_iota(jnp.int32, (chunk, rows), 1)
            peer = row // per_peer
            yc = (peer % group) * 2 + peer // group
            block = (row // PAD) % NZ
            slot = row % PAD
            rel = jnp.where(block % 2 == 1, NZ - (block + 1) // 2, block // 2)
            zz = (zi + rel) % NZ
            want = zz * (nyc * cap) + yc * cap + slot
            pick = jnp.where((col == want) & (slot < cap), 1.0, 0.0).astype(BF16)
            val = jnp.dot(pick, savedv[mb], preferred_element_type=F32)
            swapped = pltpu.roll(val, hidden, 1)
            is_gate = lax.broadcasted_iota(jnp.int32, (chunk, wide), 1) < hidden
            a = jnp.where(is_gate, val, swapped)
            u = jnp.where(is_gate, swapped, val)
            sg = jax.nn.sigmoid(a)
            silu = a * sg
            factor[mb, pl.ds(at, chunk), :] = jnp.where(
                is_gate, u * (sg * (1.0 + a * (1.0 - sg))), silu
            )
            act[pl.ds(mb * rows + at, chunk), :] = (silu * u)[:, : act.shape[1]].astype(BF16)
            return carry

        lax.fori_loop(0, half_rows // chunk, body, 0)

    def expert_stage(mb, of_core):
        at = pl.multiple_of(of_core * half_rows, half_rows)
        peers = pl.ds(of_core * group, group)
        incoming = routed[mb, peers].reshape(half_rows, width)
        grad = lax.dot_general(
            incoming, w2d[...], (((1,), (1,)), ((), ())), preferred_element_type=F32
        )
        out = (grad * factor[mb, pl.ds(at, half_rows), :]).astype(BF16)
        fog[mb, pl.ds(at, half_rows), :] = out
        back = lax.dot_general(
            out, w1v[...], (((1,), (1,)), ((), ())), preferred_element_type=F32
        ).astype(BF16)
        rsend[mb, peers] = back.reshape(group, per_peer, width)
        for pair in (3, 2, 1, 0):
            for by in range(group):
                to = ((me // 2 + by) % group) * 2 + of_core
                if by > 0:
                    r_copy(mb, pair, to).start()
                else:

                    @pl.when(of_core == core)
                    def _():
                        own_return(mb, pair).start()

                    @pl.when(of_core != core)
                    def _():
                        r_copy(mb, pair, to).start()

    def half_of(half):
        return slice(half * half_cols, (half + 1) * half_cols)

    def partial_of(at, half):
        return part[at // 2, (at % 2) * tok : (at % 2 + 1) * tok, half_of(half)]

    def combine(mb):
        def partial_sums(pair):
            wait_for(rrecv.at[mb, pair], r_recv.at[mb, pair])
            back = rrecv[mb, pair].reshape(pair_rows, width)
            part[pair] = jnp.dot(comb[mb, pair], back, preferred_element_type=F32)

        def send(slot, extra=None):
            for half in SUMS[slot][1]:
                value = partial_of(SUMS[slot][2], half)
                if extra is not None:
                    value = value + sum_recv[mb, extra[0], :, half_of(half)].astype(F32)
                    if half in SUMS[extra[1]][1]:
                        value = value + sum_recv[mb, extra[1], :, half_of(half)].astype(F32)
                sum_send[mb, slot, :, half_of(half)] = value.astype(BF16)
                q_copy(mb, slot, half).start()

        def wait_sum(slot):
            if len(SUMS[slot][1]) == 2:
                wait_for(sum_recv.at[mb, slot], q_recv.at[mb, slot])
            else:
                half = SUMS[slot][1][0]
                cols = pl.ds(half * half_cols, half_cols)
                wait_for(sum_recv.at[mb, slot, :, cols], q_recv.at[mb, slot])

        partial_sums(3)
        send(1)
        send(3)
        send(0)
        partial_sums(2)
        send(2)
        partial_sums(1)
        partial_sums(0)
        wait_sum(0)
        wait_sum(1)
        send(4, (0, 1))
        wait_sum(2)
        wait_sum(3)
        send(5, (2, 3))
        send(6)
        send(7)

    def finish(mb):
        for slot in (6, 7, 4, 5):
            wait_for(sum_recv.at[mb, slot], q_recv.at[mb, slot])
        for half in range(2):
            cols = half_of(half)
            total = gath[mb, 0, 0:tok, cols].astype(F32) + partial_of(0, half)
            for slot in (6, 7, 4, 5):
                total = total + sum_recv[mb, slot, :, cols].astype(F32)
            gout[mb, :, cols] = total.astype(BF16)

        @pl.when(pipe > 0)
        def _():
            spread_on(mb)

        sec_out[mb] = gout[mb]

    def turn_body(turn, carry):
        mb, of_core, is_chunk, is_own, is_gather, task, is_done, done_mb = plan(turn)

        @pl.when(is_gather)
        def _():
            gather(task, is_own & jnp.logical_not(is_last))

        @pl.when(turn == 0)
        def _():
            for copy in weight_copies:
                copy.wait()

            @pl.when(jnp.logical_not(is_last))
            def _():
                def body(some, carry):
                    factors(some // 2, some % 2)
                    return carry

                lax.fori_loop(0, 4, body, 0)

        @pl.when(is_chunk)
        def _():
            @pl.when(is_last)
            def _():
                factors(mb, of_core)

            wait_rows(mb, of_core)
            expert_stage(mb, of_core)

        @pl.when(is_own)
        def _():
            combine(mb)

            @pl.when(is_last)
            def _():
                @pl.when(mb == 0)
                def _():
                    spread_own(1)

                @pl.when(mb == 1)
                def _():
                    spread_own(2)
                    spread_own(3)

        @pl.when(is_done)
        def _():
            finish(done_mb)

        return carry

    lax.fori_loop(0, 8, turn_body, 0)
    for task in (2, 3):
        for of_core in range(2):
            wait_rows(task, of_core)
    both_rows = 2 * rows
    tile = 256
    grads = routed[0:2].reshape(both_rows, width)
    for start in range(0, hidden, tile):
        stop = min(start + tile, hidden)
        lanes = act[:, start : min(start + tile, act.shape[1])]
        g2 = lax.dot_general(lanes, grads, (((0,), (0,)), ((), ())), preferred_element_type=F32)
        g2_out[start:stop, :] = g2[: stop - start].astype(BF16)
    outs = fog[...].reshape(both_rows, wide)

    def g1_body(i, carry):
        at = pl.multiple_of(i * tile, tile)
        lanes = routed[2:4, :, :, pl.ds(at, tile)].reshape(both_rows, tile)
        g1 = lax.dot_general(lanes, outs, (((0,), (0,)), ((), ())), preferred_element_type=F32)
        g1_out[pl.ds(at, tile), :] = g1.astype(BF16)
        return carry

    lax.fori_loop(0, width // tile, g1_body, 0)

    @pl.when((pipe == 0) & (core == 1))
    def _():
        finish(1)

    for by in range(1, NZ):
        selection_copy(by).wait_send()
    for task in range(4):
        for sem, blocks in ((f_send, 3), (y_send, nyc - 1)):
            wait_for(sendb.at[task, pl.ds(0, blocks)], sem.at[task])
        if task >= 2:
            wait_for(sendb.at[task, pl.ds(0, 4)], d_send.at[task])

    @pl.when(is_last)
    def _():
        for mb in range(2):
            wait_for(sendb.at[mb, pl.ds(0, 4)], d_send.at[mb])

    @pl.when(pipe > 0)
    def _():
        for mb in range(2):
            wait_for(sendb.at[mb, pl.ds(0, 5)], e_send.at[mb])

    for mb in range(2):
        wait_for(sendb.at[mb, pl.ds(0, 7)], q_send.at[mb])
        wait_for(rsend.at[mb, pl.ds(0, group - 1)], r_send.at[mb, core])
        wait_for(rsend.at[mb, pl.ds(0, group)], r_send.at[mb, 1 - core])


def selection(ids, gates, experts):
    micro, tok, top = ids.shape
    flat = ids.reshape(micro, tok * top)
    order = jnp.arange(tok * top)
    earlier = (flat[:, :, None] == flat[:, None, :]) & (order[None, :] < order[:, None])[None]
    slot = jnp.sum(earlier.astype(jnp.int32), axis=2)
    target = (flat * PAD + slot).reshape(micro * tok, top)
    row = lax.broadcasted_iota(jnp.int32, (experts * PAD, micro * tok), 0)
    weight = gates.reshape(micro * tok, top)
    out = jnp.zeros((experts * PAD, micro * tok), F32)
    for k in range(top):
        out = out + jnp.where(row == target[None, :, k], weight[None, :, k], 0.0)
    return out.astype(BF16)


def per_device(cotangent, expert_ids, gates, layer_inputs, saved_fc1, w_fc1, w_fc2):
    experts = lax.axis_size("expert")
    sections = lax.axis_size("pipe")
    nyc = experts // NZ
    micro, tok, width = cotangent.shape
    slots, wide = saved_fc1.shape[3:]
    hidden = wide // 2
    cap = slots // experts
    rows = experts * PAD
    per_peer = NZ * PAD
    smat = selection(expert_ids[0], gates[0], experts)
    dims = (sections, nyc, tok, width, wide, cap)
    vmem = pl.BlockSpec(memory_space=pltpu.VMEM)
    hbm = pl.BlockSpec(memory_space=pl.ANY)
    act_width = -(-hidden // 256) * 256
    dma = pltpu.SemaphoreType.DMA
    out = pl.pallas_call(
        functools.partial(fused_kernel, dims),
        out_shape=(
            jax.ShapeDtypeStruct((micro, tok, width), BF16),
            jax.ShapeDtypeStruct((width, wide), BF16),
            jax.ShapeDtypeStruct((hidden, width), BF16),
        ),
        in_specs=[vmem, vmem, vmem, hbm, hbm, hbm],
        out_specs=(vmem, vmem, vmem),
        scratch_shapes=[
            pltpu.VMEM((4, NZ // 2, 2 * tok, width), BF16),
            pltpu.VMEM((4, nyc, per_peer, width), BF16),
            pltpu.VMEM((4, nyc, per_peer, width), BF16),
            pltpu.VMEM((2, nyc, per_peer, width), BF16),
            pltpu.VMEM((2, NZ // 2, nyc, 2 * PAD, width), BF16),
            pltpu.VMEM((NZ // 2, 2 * tok, width), F32),
            pltpu.VMEM((2, 8, tok, width), BF16),
            pltpu.VMEM((2, 8, tok, width), BF16),
            pltpu.VMEM((2, tok, width), BF16),
            pltpu.VMEM((NZ, nyc * PAD, 2 * tok), BF16),
            pltpu.VMEM((4, NZ // 2, 2 * nyc * PAD, 2 * tok), BF16),
            pltpu.VMEM((2, NZ // 2, 2 * tok, 2 * nyc * PAD), BF16),
            pltpu.VMEM((width, wide), BF16),
            pltpu.VMEM((wide, width), BF16),
            pltpu.VMEM((2, rows, wide), BF16),
            pltpu.VMEM((2, rows, wide), F32),
            pltpu.VMEM((2 * rows, act_width), BF16),
            pltpu.VMEM((2, rows, wide), BF16),
            dma((4,)),
            dma((2,)),
            dma((4,)),
            dma((4, 8, 2)),
            dma((4,)),
            dma((4, 2)),
            dma((2, 2)),
            dma((2, 4)),
            dma((2,)),
            dma((2, 8)),
            dma((NZ,)),
            dma((NZ,)),
            dma((5,)),
        ],
        compiler_params=pltpu.CompilerParams(
            collective_id=0, has_side_effects=True, vmem_limit_bytes=60 * 1024 * 1024
        ),
        name="split_backward",
    )(cotangent, smat, layer_inputs[0], saved_fc1[0, :, 0], w_fc1[0, 0], w_fc2[0, 0])
    return out[0][None], out[1][None, None], out[2][None, None]


def solution(mesh):
    in_specs = (
        P(None, "expert", None),
        P("pipe", None, "expert", None),
        P("pipe", None, "expert", None),
        P("pipe", None, "expert", None),
        P("pipe", None, "expert", None, None),
        P("pipe", "expert", None, None),
        P("pipe", "expert", None, None),
    )
    out_specs = (
        P("pipe", None, "expert", None),
        P("pipe", "expert", None, None),
        P("pipe", "expert", None, None),
    )
    return jax.shard_map(
        per_device, mesh=mesh, in_specs=in_specs, out_specs=out_specs, check_vma=False
    )
```

time: 314 us -> 265 us (0.84)
  Pallas kernels: 303 us -> 253 us
    pallas_call x1, Pallas kernels: 303 us -> 253 us  [per_device(): pl.pallas_call(functools.partial(fused_kernel, dims), out_shape=(jax.Shap...]
where the time goes in v2:
time: 265 us
  Pallas kernels  253 us (95%)
  local copies, waits for them, and re-layouts  8.75 us (3%)
    pallas_call x1, Pallas kernels, per_device(): pl.pallas_call(functools.partial(fused_kernel, dims), out_shape=(jax.Shap...  253 us
    unnamed x6, local copies, waits for them, and re-layouts  7.28 us

profile of v2, /device:TPU:1, one launch (start us, length us, event | category | flops | bytes accessed | tf_op | source)
XLA Modules:
  0.0 264.9 jit_solution(10450580923855985845)
XLA Ops:
  0.6 0.8 reshape_squeeze.4
  1.4 0.7 broadcast_multiply_fusion
  2.1 0.1 copy.14
  2.2 0.8 copy.15
  3.0 0.1 eq.75
  3.2 0.4 convert_reduce_fusion
  3.6 0.1 reduce_sum.12
  3.8 0.3 slice_reduce_fusion.5
  4.1 0.8 add_convert_fusion.smat
  4.9 253.5 %split_backward.1 = (bf16[2,64,1024]{2,1,0:T(8,128)(2,1)}, bf16[1024,1408]{1,0:T(8,128)(2,1)}, bf16[704,1024]{1,0:T(8,128)(2,1)}) custom-call(bf16[2,64,1024]{2,1,0:T(8,128)(2,1)} %cot.1, bf16[512,128]{1,0:T(8,128)(2,1)} %add_convert_fusion.smat, bf16[2,64,1024]{2,1,0:T(8,128)(2,1)} %bitcast.29, bf16[2,448,1408]{2,1,0:T(8,128)(2,1)} %bitcast.26, ...), custom_call_target="tpu_custom_call" | custom-call | tf_op jit(solution)/shard_map/split_backward/pallas_call | solution.py:570
  258.4 1.7 copy.19
  260.1 0.0 copy-start
  260.1 3.7 %copy.20 = bf16[1,1,1024,1408]{3,2,1,0:T(8,128)(2,1)} copy(bf16[1,1,1024,1408]{3,2,1,0:T(8,128)(2,1)} %bitcast.25) | data formatting | bytes 5767168
  263.8 0.0 copy-done
  263.8 1.1 copy.21
  (3 shorter events, 0.1 us)
Async XLA Ops:
  260.1 3.7 %copy-start = (bf16[704,1024]{1,0:T(8,128)(2,1)S(1)}, bf16[704,1024]{1,0:T(8,128)(2,1)}, u32[]{:S(2)}) copy-start(bf16[704,1024]{1,0:T(8,128)(2,1)} %get-tuple-element.8) | copy-start | bytes 4325380

commit v3 on v2

v3 whole, which is shorter than its diff:
```python
import functools

import jax
import jax.numpy as jnp
from jax import lax
from jax.experimental import pallas as pl
from jax.experimental.pallas import tpu as pltpu
from jax.sharding import PartitionSpec as P

MESH = pl.DeviceIdType.MESH
NZ = 8
PAD = 8
F32, BF16 = jnp.float32, jnp.bfloat16


SUMS = {
    0: (1, (0, 1), 6),
    1: (2, (0,), 7),
    2: (-1, (0, 1), 5),
    3: (-2, (1,), 7),
    4: (2, (0, 1), 4),
    5: (-2, (0, 1), 3),
    6: (1, (0, 1), 2),
    7: (-1, (0, 1), 1),
}


def fused_kernel(
    dims,
    cot,
    ids,
    gates,
    xin,
    saved_hbm,
    w1_hbm,
    w2_hbm,
    sec_out,
    g1_out,
    g2_out,
    gath,
    sendb,
    routed,
    rsend,
    rrecv,
    part,
    sum_send,
    sum_recv,
    gout,
    stage,
    smat,
    srecv,
    sel,
    comb,
    w1v,
    w2d,
    savedv,
    factor,
    act,
    fog,
    d_send,
    e_send,
    f_send,
    z_recv,
    y_send,
    y_recv,
    r_send,
    r_recv,
    q_send,
    q_recv,
    s_send,
    s_recv,
    o_send,
    o_recv,
    h_send,
    local_sem,
):
    sections, nyc, tok, width, wide, cap = dims
    hidden = wide // 2
    side = width // 2
    half_cols = side // 2
    rows_in = NZ * nyc * cap
    rows = NZ * nyc * PAD
    per_peer = NZ * PAD
    pair_rows = 2 * nyc * PAD
    sel_rows = nyc * PAD
    group = nyc // 2

    pipe = lax.axis_index("pipe")
    expert = lax.axis_index("expert")
    zi = expert // nyc
    me = expert % nyc
    core = me % 2

    other = 1 - core
    sibling = me + 1 - 2 * core

    def along_z(by, plane=None, to=None):
        at = ((zi + by + NZ) % NZ) * nyc + (me if to is None else to)
        return (pipe if plane is None else plane, at)

    def along_y(yc):
        return (pipe, zi * nyc + yc)

    is_last = pipe == sections - 1
    before = (pipe + sections - 1) % sections
    after = (pipe + 1) % sections

    weight_copies = (
        pltpu.make_async_copy(w1_hbm, w1v, local_sem.at[0]),
        pltpu.make_async_copy(w2_hbm, w2d.at[pl.ds(0, hidden), :], local_sem.at[1]),
        pltpu.make_async_copy(w2_hbm, w2d.at[pl.ds(hidden, hidden), :], local_sem.at[2]),
        pltpu.make_async_copy(saved_hbm.at[0], savedv.at[0, pl.ds(0, rows_in), :], local_sem.at[3]),
        pltpu.make_async_copy(saved_hbm.at[1], savedv.at[1, pl.ds(0, rows_in), :], local_sem.at[4]),
    )

    barrier = pltpu.get_barrier_semaphore()
    for by in range(1, NZ):
        pl.semaphore_signal(barrier, inc=1, device_id=along_z(by), device_id_type=MESH)
        pl.semaphore_signal(
            barrier, inc=1, device_id=along_z(by, to=sibling), device_id_type=MESH
        )
    for by in range(1, nyc):
        pl.semaphore_signal(
            barrier, inc=1, device_id=along_y((me + by) % nyc), device_id_type=MESH
        )
    for by in range(-2, 3):
        for plane in (before, after):
            pl.semaphore_signal(
                barrier, inc=1, device_id=along_z(by, plane), device_id_type=MESH
            )

    for copy in weight_copies:
        copy.start()
    for mb in range(2):
        if rows > rows_in:
            savedv[mb, rows_in:rows, :] = jnp.zeros((rows - rows_in, wide), BF16)

    experts = NZ * nyc
    lanes_two = 2 * tok
    named = lax.broadcasted_iota(jnp.int32, (experts, lanes_two), 0)
    hit = jnp.zeros((experts, lanes_two), F32)
    weight = jnp.zeros((experts, lanes_two), F32)
    for k in range(ids.shape[0]):
        of_k = jnp.concatenate([ids[k, 0:1, :], ids[k, 1:2, :]], axis=1)
        gate_k = jnp.concatenate([gates[k, 0:1, :], gates[k, 1:2, :]], axis=1)
        same = named == of_k
        hit = hit + jnp.where(same, 1.0, 0.0)
        weight = weight + jnp.where(same, gate_k, 0.0)
    first = lax.broadcasted_iota(jnp.int32, (lanes_two, lanes_two), 0)
    second = lax.broadcasted_iota(jnp.int32, (lanes_two, lanes_two), 1)
    earlier = (first < second) & ((first < tok) == (second < tok))
    rank = jnp.dot(
        hit.astype(BF16),
        jnp.where(earlier, 1.0, 0.0).astype(BF16),
        preferred_element_type=F32,
    ).astype(jnp.int32)
    slot_no = lax.broadcasted_iota(jnp.int32, (experts, PAD, lanes_two), 1)
    spread_out = jnp.where(rank[:, None, :] == slot_no, weight[:, None, :], 0.0)
    smat[...] = spread_out.reshape(experts * PAD, lanes_two).astype(BF16)

    my_cols = pl.ds(pl.multiple_of(core * side, side), side)
    for mb in range(2):
        gath[2 + mb, core, 0, 0:tok, :] = xin[mb, :, my_cols]

    @pl.when(is_last)
    def _():
        for mb in range(2):
            gath[mb, core, 0, 0:tok, :] = cot[mb, :, my_cols]

    pltpu.make_async_copy(
        smat.at[pl.ds(pl.multiple_of(zi * sel_rows, sel_rows), sel_rows), :],
        srecv.at[core, 0],
        s_recv,
    ).start()
    pl.semaphore_wait(barrier, 2 * (NZ - 1) + nyc - 1 + 10)

    def wait_for(ref, sem):
        pltpu.make_async_copy(ref, ref, sem).wait()

    def selection_copy(by, swap):
        at = 0 if by == 0 else 2 * by - 1 if by <= 4 else 2 * (NZ - by)
        to = (zi + by) % NZ
        return pltpu.make_async_remote_copy(
            src_ref=smat.at[pl.ds(pl.multiple_of(to * sel_rows, sel_rows), sel_rows), :],
            dst_ref=srecv.at[core, at],
            send_sem=s_send.at[1 if swap else 0],
            recv_sem=s_recv,
            device_id=along_z(by, to=sibling if swap else me),
            device_id_type=MESH,
        )

    def block_view(task, of, at, half):
        return gath.at[
            task,
            of,
            at // 2,
            pl.ds((at % 2) * tok, tok),
            pl.ds(half * half_cols, half_cols),
        ]

    def spread_copy(src, task, of, by, at, half, sem, plane=None):
        return pltpu.make_async_remote_copy(
            src_ref=src,
            dst_ref=block_view(task, of, at, half),
            send_sem=sem,
            recv_sem=z_recv.at[task, of, at, half],
            device_id=along_z(by, plane),
            device_id_type=MESH,
        )

    def wait_block(task, of, at, half):
        wait_for(block_view(task, of, at, half), z_recv.at[task, of, at, half])

    def hand_over(source, mb, task):
        for half in range(2):
            at = pl.multiple_of(other * side + half * half_cols, half_cols)
            pltpu.make_async_remote_copy(
                src_ref=source.at[mb, :, pl.ds(at, half_cols)],
                dst_ref=block_view(task, core, 0, half),
                send_sem=h_send.at[task],
                recv_sem=z_recv.at[task, core, 0, half],
                device_id=along_y(sibling),
                device_id_type=MESH,
            ).start()

    def spread_own(task, of):
        @pl.when(other == of)
        def _():
            for half in range(2):
                wait_block(task, of, 0, half)

        for by, at in ((2, 3), (-2, 4), (1, 1), (-1, 2)):
            for half in range(2):
                src = block_view(task, of, 0, half)
                spread_copy(src, task, of, by, at, half, d_send.at[task, of]).start()

    def spread_on(mb, of):
        for by, at in ((2, 3), (-2, 4), (1, 1), (-1, 2), (0, 0)):
            for half in range(2):
                src = gout.at[mb, of, :, pl.ds(half * half_cols, half_cols)]
                spread_copy(src, mb, of, by, at, half, e_send.at[mb, of], before).start()

    def y_copy(task, of, by, at, count):
        to = (me + by) % nyc
        return pltpu.make_async_remote_copy(
            src_ref=sendb.at[task, of, to, pl.ds(at, count), :],
            dst_ref=routed.at[task, core, of * group + me // 2, pl.ds(at, count), :],
            send_sem=y_send.at[task, of],
            recv_sem=y_recv.at[task, of],
            device_id=along_y(to),
            device_id_type=MESH,
        )

    def own_copy(task, of):
        return pltpu.make_async_copy(
            sendb.at[task, of, me],
            routed.at[task, core, of * group + me // 2],
            y_recv.at[task, of],
        )

    def wait_rows(task, of):
        here = routed.at[task, :, pl.ds(of * group, group)]
        wait_for(here, y_recv.at[task, of])

    def r_copy(mb, of, pair, to):
        return pltpu.make_async_remote_copy(
            src_ref=rsend.at[mb, to % 2, of * group + to // 2, pl.ds(pair * 2 * PAD, 2 * PAD), :],
            dst_ref=rrecv.at[mb, of, pair, me],
            send_sem=r_send.at[mb, of],
            recv_sem=r_recv.at[mb, of, pair],
            device_id=along_y(to),
            device_id_type=MESH,
        )

    def own_return(mb, of, pair):
        return pltpu.make_async_copy(
            rsend.at[mb, core, of * group + me // 2, pl.ds(pair * 2 * PAD, 2 * PAD), :],
            rrecv.at[mb, of, pair, me],
            r_recv.at[mb, of, pair],
        )

    def q_copy(mb, of, slot, half):
        cols = pl.ds(half * half_cols, half_cols)
        return pltpu.make_async_remote_copy(
            src_ref=sum_send.at[mb, of, slot, :, cols],
            dst_ref=sum_recv.at[mb, of, slot, :, cols],
            send_sem=q_send.at[mb, of],
            recv_sem=q_recv.at[mb, of, slot],
            device_id=along_z(SUMS[slot][0]),
            device_id_type=MESH,
        )

    def plan(turn):
        chunk_no = turn - 4
        is_chunk = (turn >= 4) & (turn < 8)
        of = turn % 2
        mb = jnp.where(is_chunk, chunk_no // 2, 0)
        is_x = ((turn < 4) & jnp.logical_not(is_last)) | ((turn >= 10) & is_last)
        x_no = jnp.where(turn < 4, turn, turn - 10)
        task = jnp.where(is_chunk, mb, 2 + x_no // 2)
        gather_of = jnp.where(is_chunk, of, x_no % 2)
        is_back = (turn >= 5) & (turn <= 8)
        back_mb = jnp.where(is_back, (turn - 5) // 2, 0)
        is_end = (turn >= 6) & (turn <= 9)
        end_mb = jnp.where(is_end, (turn - 6) // 2, 0)
        back = (is_back, back_mb, (turn + 1) % 2)
        return mb, of, is_chunk, is_chunk | is_x, task, gather_of, back, (is_end, end_mb, of)

    @pl.when(is_last)
    def _():
        hand_over(cot, 0, 0)
        spread_own(0, 0)
        hand_over(cot, 1, 1)

    hand_over(xin, 0, 2)
    hand_over(xin, 1, 3)
    for by in range(NZ):
        for swap in (True, False):
            if by > 0 or swap:
                selection_copy(by, swap).start()

    @pl.when(jnp.logical_not(is_last))
    def _():
        for no in range(4):
            spread_own(2 + no // 2, no % 2)

    lane = lax.broadcasted_iota(jnp.int32, (sel_rows, 2 * tok), 1)
    low = lane < tok
    wait_for(srecv, s_recv)

    def build(of, carry):
        for pair in range(NZ // 2):
            first, second = srecv[of, 2 * pair].astype(F32), srecv[of, 2 * pair + 1].astype(F32)
            for mb in range(2):
                one = first if mb == 0 else pltpu.roll(first, tok, 1)
                two = second if mb == 1 else pltpu.roll(second, tok, 1)
                one = jnp.where(low, one, 0.0)
                two = jnp.where(low, 0.0, two)
                pieces = []
                for yc in range(nyc):
                    pieces += [one[yc * PAD : (yc + 1) * PAD], two[yc * PAD : (yc + 1) * PAD]]
                both = jnp.concatenate(pieces, axis=0)
                ones = jnp.where(both != 0.0, 1.0, 0.0)
                sel[mb, of, pair] = both.astype(BF16)
                sel[2 + mb, of, pair] = ones.astype(BF16)
                comb[mb, of, pair] = ones.T.astype(BF16)
        return carry

    lax.fori_loop(0, 2, build, 0)

    @pl.when(is_last)
    def _():
        spread_own(0, 1)

    def select(task, of, pair):
        chosen = jnp.dot(
            sel[task, of, pair], gath[task, of, pair], preferred_element_type=F32
        ).astype(BF16)
        at = pair * 2 * PAD
        for yc in range(nyc):
            sendb[task, of, yc, at : at + 2 * PAD, :] = chosen[yc * 2 * PAD : (yc + 1) * 2 * PAD]
        for by in range(1, nyc):
            y_copy(task, of, by, at, 2 * PAD).start()

    def gather(task, of, is_handed_on):
        def forward(from_at, by, at, half):
            src = block_view(task, of, from_at, half)
            spread_copy(src, task, of, by, at, half, f_send.at[task, of]).start()

        wait_block(task, of, 3, 0)
        forward(3, 2, 7, 0)
        forward(3, 1, 5, 0)
        wait_block(task, of, 4, 1)
        forward(4, -2, 7, 1)
        forward(4, -1, 6, 1)
        wait_block(task, of, 3, 1)
        forward(3, 1, 5, 1)
        wait_block(task, of, 4, 0)
        forward(4, -1, 6, 0)
        for half in range(2):
            wait_block(task, of, 1, half)

        @pl.when(is_handed_on)
        def _():
            for half in range(2):
                wait_block(task, of, 0, half)

        select(task, of, 0)
        for half in range(2):
            wait_block(task, of, 2, half)
        select(task, of, 1)

    def gather_rest(task, of):
        for pair, needs in ((2, (5,)), (3, (6, 7))):
            for at in needs:
                for half in range(2):
                    wait_block(task, of, at, half)
            select(task, of, pair)
        own_copy(task, of).start()

    chunk = min(128, rows)

    half_rows = rows // 2

    def factors(mb, of_core):
        def body(i, carry):
            at = pl.multiple_of(of_core * half_rows + i * chunk, chunk)
            row = lax.broadcasted_iota(jnp.int32, (chunk, rows), 0) + at
            col = lax.broadcasted_iota(jnp.int32, (chunk, rows), 1)
            peer = row // per_peer
            yc = (peer % group) * 2 + peer // group
            block = (row // PAD) % NZ
            slot = row % PAD
            rel = jnp.where(block % 2 == 1, NZ - (block + 1) // 2, block // 2)
            zz = (zi + rel) % NZ
            want = zz * (nyc * cap) + yc * cap + slot
            pick = jnp.where((col == want) & (slot < cap), 1.0, 0.0).astype(BF16)
            val = jnp.dot(pick, savedv[mb], preferred_element_type=F32)
            swapped = pltpu.roll(val, hidden, 1)
            is_gate = lax.broadcasted_iota(jnp.int32, (chunk, wide), 1) < hidden
            a = jnp.where(is_gate, val, swapped)
            u = jnp.where(is_gate, swapped, val)
            sg = jax.nn.sigmoid(a)
            silu = a * sg
            factor[mb, pl.ds(at, chunk), :] = jnp.where(
                is_gate, u * (sg * (1.0 + a * (1.0 - sg))), silu
            )
            act[pl.ds(mb * rows + at, chunk), :] = (silu * u)[:, : act.shape[1]].astype(BF16)
            return carry

        lax.fori_loop(0, half_rows // chunk, body, 0)

    def expert_stage(mb, of):
        at = pl.multiple_of(of * half_rows, half_rows)
        peers = pl.ds(of * group, group)
        grad = jnp.zeros((half_rows, wide), F32)
        for k in range(2):
            incoming = routed[mb, k, peers].reshape(half_rows, side)
            grad = grad + lax.dot_general(
                incoming,
                w2d[:, k * side : (k + 1) * side],
                (((1,), (1,)), ((), ())),
                preferred_element_type=F32,
            )
        out = (grad * factor[mb, pl.ds(at, half_rows), :]).astype(BF16)
        fog[mb, pl.ds(at, half_rows), :] = out
        for k in range(2):
            back = lax.dot_general(
                out,
                w1v[k * side : (k + 1) * side, :],
                (((1,), (1,)), ((), ())),
                preferred_element_type=F32,
            ).astype(BF16)
            rsend[mb, k, peers] = back.reshape(group, per_peer, side)
        for pair in (3, 2, 1, 0):
            own_return(mb, of, pair).start()
            for by in range(1, nyc):
                r_copy(mb, of, pair, (me + by) % nyc).start()

    def half_of(half):
        return slice(half * half_cols, (half + 1) * half_cols)

    def partial_of(of, at, half):
        return part[of, at // 2, (at % 2) * tok : (at % 2 + 1) * tok, half_of(half)]

    def sender(mb, of):
        def send(slot, extra=None):
            for half in SUMS[slot][1]:
                value = partial_of(of, SUMS[slot][2], half)
                if extra is not None:
                    value = value + sum_recv[mb, of, extra[0], :, half_of(half)].astype(F32)
                    if half in SUMS[extra[1]][1]:
                        value = value + sum_recv[mb, of, extra[1], :, half_of(half)].astype(F32)
                sum_send[mb, of, slot, :, half_of(half)] = value.astype(BF16)
                q_copy(mb, of, slot, half).start()

        def wait_sum(slot):
            if len(SUMS[slot][1]) == 2:
                wait_for(sum_recv.at[mb, of, slot], q_recv.at[mb, of, slot])
            else:
                half = SUMS[slot][1][0]
                cols = pl.ds(half * half_cols, half_cols)
                wait_for(sum_recv.at[mb, of, slot, :, cols], q_recv.at[mb, of, slot])

        return send, wait_sum

    def combine(mb, of):
        def partial_sums(pair):
            wait_for(rrecv.at[mb, of, pair], r_recv.at[mb, of, pair])
            back = rrecv[mb, of, pair].reshape(pair_rows, side)
            part[of, pair] = jnp.dot(comb[mb, of, pair], back, preferred_element_type=F32)

        send, _ = sender(mb, of)
        partial_sums(3)
        send(1)
        send(3)
        send(0)
        partial_sums(2)
        send(2)
        partial_sums(1)
        partial_sums(0)
        send(6)
        send(7)

    def hand_sums_on(mb, of):
        send, wait_sum = sender(mb, of)
        wait_sum(0)
        wait_sum(1)
        send(4, (0, 1))
        wait_sum(2)
        wait_sum(3)
        send(5, (2, 3))

    def stage_copy(mb):
        return pltpu.make_async_remote_copy(
            src_ref=gout.at[mb, other],
            dst_ref=stage.at[mb, core],
            send_sem=o_send.at[mb],
            recv_sem=o_recv.at[mb],
            device_id=along_y(sibling),
            device_id_type=MESH,
        )

    def finish(mb, of):
        for slot in (6, 7, 4, 5):
            wait_for(sum_recv.at[mb, of, slot], q_recv.at[mb, of, slot])
        total = gath[mb, of, 0, 0:tok, :].astype(F32) + part[of, 0, 0:tok, :]
        for slot in (6, 7, 4, 5):
            total = total + sum_recv[mb, of, slot].astype(F32)
        total = total.astype(BF16)
        gout[mb, of] = total

        @pl.when(pipe > 0)
        def _():
            spread_on(mb, of)

        @pl.when(of == core)
        def _():
            stage[mb, core] = total

        @pl.when(of != core)
        def _():
            stage_copy(mb).start()

    def turn_body(turn, carry):
        mb, of, is_chunk, is_gather, task, gather_of, back, end = plan(turn)

        @pl.when(is_gather)
        def _():
            gather(task, gather_of, is_chunk & jnp.logical_not(is_last))

        @pl.when(end[0] & jnp.logical_not((turn == 9) & (pipe == 0)))
        def _():
            finish(end[1], end[2])

        @pl.when(back[0])
        def _():
            combine(back[1], back[2])

        @pl.when(is_gather)
        def _():
            gather_rest(task, gather_of)

        @pl.when(is_last)
        def _():
            for at, chunks in ((5, ((1, 0),)), (6, ((1, 1),)), (8, ((2, 0), (2, 1))), (9, ((3, 0), (3, 1)))):

                @pl.when(turn == at)
                def _():
                    for chunk_at in chunks:
                        spread_own(*chunk_at)

        @pl.when(turn == 3)
        def _():
            for copy in weight_copies:
                copy.wait()

            @pl.when(jnp.logical_not(is_last))
            def _():
                def some_factors(some, carry):
                    factors(some // 2, some % 2)
                    return carry

                lax.fori_loop(0, 4, some_factors, 0)

        @pl.when(is_chunk)
        def _():
            @pl.when(is_last)
            def _():
                factors(mb, of)

            wait_rows(mb, of)
            expert_stage(mb, of)

        @pl.when(back[0])
        def _():
            hand_sums_on(back[1], back[2])

        return carry

    lax.fori_loop(0, 14, turn_body, 0)
    for task in (2, 3):
        for of in range(2):
            wait_rows(task, of)

    both_rows = 2 * rows
    tile = 256
    for start in range(0, hidden, tile):
        stop = min(start + tile, hidden)
        lanes = act[:, start : min(start + tile, act.shape[1])]
        for k in range(2):
            grads = routed[0:2, k].reshape(both_rows, side)
            g2 = lax.dot_general(lanes, grads, (((0,), (0,)), ((), ())), preferred_element_type=F32)
            g2_out[start:stop, k * side : (k + 1) * side] = g2[: stop - start].astype(BF16)
    outs = fog[...].reshape(both_rows, wide)

    def g1_body(i, carry):
        at = pl.multiple_of(i * tile, tile)
        col = pl.multiple_of((i % (side // tile)) * tile, tile)
        lanes = routed[2:4, i // (side // tile), :, :, pl.ds(col, tile)].reshape(both_rows, tile)
        g1 = lax.dot_general(lanes, outs, (((0,), (0,)), ((), ())), preferred_element_type=F32)
        g1_out[pl.ds(at, tile), :] = g1.astype(BF16)
        return carry

    lax.fori_loop(0, width // tile, g1_body, 0)

    @pl.when(pipe == 0)
    def _():
        finish(1, 1)

    for mb in range(2):
        stage_copy(mb).wait_recv()
        for k in range(2):
            sec_out[mb, :, k * side : (k + 1) * side] = stage[mb, k]

    def left(blocks, sem):
        wait_for(sendb.at[0, 0, pl.ds(0, blocks)], sem)

    wait_for(srecv.at[0, pl.ds(0, NZ - 1)], s_send.at[0])
    wait_for(srecv.at[0], s_send.at[1])
    for task in range(4):
        for of in range(2):
            left(3, f_send.at[task, of])
            left(nyc - 1, y_send.at[task, of])
            if task >= 2:
                left(4, d_send.at[task, of])
        if task >= 2:
            left(1, h_send.at[task])

    @pl.when(is_last)
    def _():
        for mb in range(2):
            left(1, h_send.at[mb])
            for of in range(2):
                left(4, d_send.at[mb, of])

    @pl.when(pipe > 0)
    def _():
        for mb in range(2):
            for of in range(2):
                left(5, e_send.at[mb, of])

    for mb in range(2):
        stage_copy(mb).wait_send()
        for of in range(2):
            left(7, q_send.at[mb, of])
            left(nyc - 1, r_send.at[mb, of])


def copy_kernel(parts, *refs):
    count = len(parts)
    in_sem, out_sem = refs[-2:]
    pairs = []
    for at in range(count):
        source, target, held = refs[at], refs[count + at], refs[2 * count + at]
        rows = source.shape[0] // parts[at]
        for piece in range(parts[at]):
            here = pl.ds(piece * rows, rows)
            no = len(pairs)
            pairs.append(
                (
                    pltpu.make_async_copy(source.at[here], held.at[here], in_sem.at[no]),
                    pltpu.make_async_copy(held.at[here], target.at[here], out_sem.at[no]),
                )
            )
    for bring, _ in pairs:
        bring.start()
    for bring, put in pairs:
        bring.wait()
        put.start()
    for _, put in pairs:
        put.wait()


def per_device(cotangent, expert_ids, gates, layer_inputs, saved_fc1, w_fc1, w_fc2):
    experts = lax.axis_size("expert")
    sections = lax.axis_size("pipe")
    nyc = experts // NZ
    micro, tok, width = cotangent.shape
    slots, wide = saved_fc1.shape[3:]
    hidden = wide // 2
    cap = slots // experts
    rows = experts * PAD
    per_peer = NZ * PAD
    side = width // 2
    dims = (sections, nyc, tok, width, wide, cap)
    vmem = pl.BlockSpec(memory_space=pltpu.VMEM)
    hbm = pl.BlockSpec(memory_space=pl.ANY)
    act_width = -(-hidden // 256) * 256
    dma = pltpu.SemaphoreType.DMA
    out = pl.pallas_call(
        functools.partial(fused_kernel, dims),
        out_shape=(
            jax.ShapeDtypeStruct((micro, tok, width), BF16),
            jax.ShapeDtypeStruct((width, wide), BF16),
            jax.ShapeDtypeStruct((hidden, width), BF16),
        ),
        in_specs=[vmem, vmem, vmem, vmem, hbm, hbm, hbm],
        out_specs=(vmem, vmem, vmem),
        scratch_shapes=[
            pltpu.VMEM((4, 2, NZ // 2, 2 * tok, side), BF16),
            pltpu.VMEM((4, 2, nyc, per_peer, side), BF16),
            pltpu.VMEM((4, 2, nyc, per_peer, side), BF16),
            pltpu.VMEM((2, 2, nyc, per_peer, side), BF16),
            pltpu.VMEM((2, 2, NZ // 2, nyc, 2 * PAD, side), BF16),
            pltpu.VMEM((2, NZ // 2, 2 * tok, side), F32),
            pltpu.VMEM((2, 2, 8, tok, side), BF16),
            pltpu.VMEM((2, 2, 8, tok, side), BF16),
            pltpu.VMEM((2, 2, tok, side), BF16),
            pltpu.VMEM((2, 2, tok, side), BF16),
            pltpu.VMEM((experts * PAD, 2 * tok), BF16),
            pltpu.VMEM((2, NZ, nyc * PAD, 2 * tok), BF16),
            pltpu.VMEM((4, 2, NZ // 2, 2 * nyc * PAD, 2 * tok), BF16),
            pltpu.VMEM((2, 2, NZ // 2, 2 * tok, 2 * nyc * PAD), BF16),
            pltpu.VMEM((width, wide), BF16),
            pltpu.VMEM((wide, width), BF16),
            pltpu.VMEM((2, rows, wide), BF16),
            pltpu.VMEM((2, rows, wide), F32),
            pltpu.VMEM((2 * rows, act_width), BF16),
            pltpu.VMEM((2, rows, wide), BF16),
            dma((4, 2)),
            dma((2, 2)),
            dma((4, 2)),
            dma((4, 2, 8, 2)),
            dma((4, 2)),
            dma((4, 2)),
            dma((2, 2)),
            dma((2, 2, 4)),
            dma((2, 2)),
            dma((2, 2, 8)),
            dma((2,)),
            dma(()),
            dma((2,)),
            dma((2,)),
            dma((4,)),
            dma((5,)),
        ],
        compiler_params=pltpu.CompilerParams(
            collective_id=0, has_side_effects=True, vmem_limit_bytes=60 * 1024 * 1024
        ),
        name="split_backward",
    )(
        cotangent,
        expert_ids[0].transpose(2, 0, 1),
        gates[0].transpose(2, 0, 1),
        layer_inputs[0],
        saved_fc1[0, :, 0],
        w_fc1[0, 0],
        w_fc2[0, 0],
    )
    parts = (2, 8, 4)
    out = pl.pallas_call(
        functools.partial(copy_kernel, parts),
        out_shape=tuple(jax.ShapeDtypeStruct(o.shape, o.dtype) for o in out),
        in_specs=[hbm] * 3,
        out_specs=(hbm,) * 3,
        scratch_shapes=[
            *(pltpu.VMEM(o.shape, o.dtype) for o in out),
            dma((sum(parts),)),
            dma((sum(parts),)),
        ],
        compiler_params=pltpu.CompilerParams(vmem_limit_bytes=60 * 1024 * 1024),
        name="copy_out",
    )(*out)
    return out[0][None], out[1][None, None], out[2][None, None]


def solution(mesh):
    in_specs = (
        P(None, "expert", None),
        P("pipe", None, "expert", None),
        P("pipe", None, "expert", None),
        P("pipe", None, "expert", None),
        P("pipe", None, "expert", None, None),
        P("pipe", "expert", None, None),
        P("pipe", "expert", None, None),
    )
    out_specs = (
        P("pipe", None, "expert", None),
        P("pipe", "expert", None, None),
        P("pipe", "expert", None, None),
    )
    return jax.shard_map(
        per_device, mesh=mesh, in_specs=in_specs, out_specs=out_specs, check_vma=False
    )
```

time: 265 us -> 250 us (0.943)
  local copies, waits for them, and re-layouts: 8.75 us -> 0 us
  Pallas kernels: 253 us -> 250 us
    pallas_call x1, Pallas kernels: 253 us -> 245 us  [per_device(): pl.pallas_call(functools.partial(fused_kernel, dims), out_shape=(jax.Shap...]
    unnamed x6 -> x0, local copies, waits for them, and re-layouts: 7.28 us -> none
    pallas_call x0 -> x1, Pallas kernels: none -> 4.34 us  [per_device(): pl.pallas_call(functools.partial(copy_kernel, parts), out_shape=tuple((ja...]
where the time goes in v3:
time: 250 us
  Pallas kernels  250 us (100%)
    pallas_call x1, Pallas kernels, per_device(): pl.pallas_call(functools.partial(fused_kernel, dims), out_shape=(jax.Shap...  245 us

profile of v3, /device:TPU:1, one launch (start us, length us, event | category | flops | bytes accessed | tf_op | source)
XLA Modules:
  0.0 250.1 jit_solution(17867422209985104713)
XLA Ops:
  0.6 245.2 %split_backward.1 = (bf16[2,64,1024]{2,1,0:T(8,128)(2,1)}, bf16[1024,1408]{1,0:T(8,128)(2,1)}, bf16[704,1024]{1,0:T(8,128)(2,1)}) custom-call(bf16[2,64,1024]{2,1,0:T(8,128)(2,1)} %cot.1, s32[6,2,64]{2,1,0:T(2,128)} %bitcast.17, f32[6,2,64]{2,1,0:T(2,128)} %bitcast.18, bf16[2,64,1024]{2,1,0:T(8,128)(2,1)} %bitcast.16, bf16[2,448,1408]{2,1,0:T(8,128)(2,1)} %bitcast.14, ...), custom_call_target="tpu_custom_call" | custom-call | tf_op jit(solution)/shard_map/split_backward/pallas_call | solution.py:711
  245.8 4.3 %copy_out.1 = (bf16[2,64,1024]{2,1,0:T(8,128)(2,1)}, bf16[1024,1408]{1,0:T(8,128)(2,1)}, bf16[704,1024]{1,0:T(8,128)(2,1)}) custom-call(bf16[2,64,1024]{2,1,0:T(8,128)(2,1)} %get-tuple-element.9.refs_0_, bf16[1024,1408]{1,0:T(8,128)(2,1)} %get-tuple-element.10.refs_1_, bf16[704,1024]{1,0:T(8,128)(2,1)} %get-tuple-element.11.refs_2_), custom_call_target="tpu_custom_call" | custom-call | tf_op jit(solution)/shard_map/copy_out/pallas_call | solution.py:772

commit v4 on v3

--- a/solution.py
+++ b/solution.py
@@ -561,6 +561,10 @@
         def _():
             gather_rest(task, gather_of)
 
+        @pl.when(back[0])
+        def _():
+            hand_sums_on(back[1], back[2])
+
         @pl.when(is_last)
         def _():
             for at, chunks in ((5, ((1, 0),)), (6, ((1, 1),)), (8, ((2, 0), (2, 1))), (9, ((3, 0), (3, 1)))):
@@ -591,10 +595,6 @@
 
             wait_rows(mb, of)
             expert_stage(mb, of)
-
-        @pl.when(back[0])
-        def _():
-            hand_sums_on(back[1], back[2])
 
         return carry
 

time: 250 us -> 241 us (0.964)
  Pallas kernels: 250 us -> 240 us
    pallas_call x1, Pallas kernels: 245 us -> 236 us  [per_device(): pl.pallas_call(functools.partial(fused_kernel, dims), out_shape=(jax.Shap...]
where the time goes in v4:
time: 241 us
  Pallas kernels  240 us (100%)
    pallas_call x1, Pallas kernels, per_device(): pl.pallas_call(functools.partial(fused_kernel, dims), out_shape=(jax.Shap...  236 us

profile of v4, /device:TPU:1, one launch (start us, length us, event | category | flops | bytes accessed | tf_op | source)
XLA Modules:
  0.0 240.9 jit_solution(12333037812892425941)
XLA Ops:
  0.6 235.9 %split_backward.1 = (bf16[2,64,1024]{2,1,0:T(8,128)(2,1)}, bf16[1024,1408]{1,0:T(8,128)(2,1)}, bf16[704,1024]{1,0:T(8,128)(2,1)}) custom-call(bf16[2,64,1024]{2,1,0:T(8,128)(2,1)} %cot.1, s32[6,2,64]{2,1,0:T(2,128)} %bitcast.17, f32[6,2,64]{2,1,0:T(2,128)} %bitcast.18, bf16[2,64,1024]{2,1,0:T(8,128)(2,1)} %bitcast.16, bf16[2,448,1408]{2,1,0:T(8,128)(2,1)} %bitcast.14, ...), custom_call_target="tpu_custom_call" | custom-call | tf_op jit(solution)/shard_map/split_backward/pallas_call | solution.py:711
  236.5 4.3 %copy_out.1 = (bf16[2,64,1024]{2,1,0:T(8,128)(2,1)}, bf16[1024,1408]{1,0:T(8,128)(2,1)}, bf16[704,1024]{1,0:T(8,128)(2,1)}) custom-call(bf16[2,64,1024]{2,1,0:T(8,128)(2,1)} %get-tuple-element.9.refs_0_, bf16[1024,1408]{1,0:T(8,128)(2,1)} %get-tuple-element.10.refs_1_, bf16[704,1024]{1,0:T(8,128)(2,1)} %get-tuple-element.11.refs_2_), custom_call_target="tpu_custom_call" | custom-call | tf_op jit(solution)/shard_map/copy_out/pallas_call | solution.py:772
